TPU v7x, 128 devices: a whole 4x4x4 slice. The times are simulated.
128 devices in a mesh: seq: 32 (over z_hi, y, x), tp: 4 (over z_lo, core).
Axes of the slice: x: 4, y: 4, z: 4 (z_hi: 2, z_lo: 2; z = z_hi * 2 + z_lo), core: 2. Of those that a mesh axis runs over, the one named last changes fastest.
Arguments:
- tokens: bfloat16 [12288, 5376], P('seq', 'tp'), may hold values from -6 to 6
- positions: int32 [12288], P('seq'), may hold values from 0 to 2047, as said below
- w_query: bfloat16 [5376, 3072], P(None, 'tp'), may hold values from -0.078125 to 0.078125
- w_key: bfloat16 [5376, 1536], P(None, 'tp'), may hold values from -0.078125 to 0.078125
- w_value: bfloat16 [5376, 1536], P(None, 'tp'), may hold values from -0.078125 to 0.078125
- w_out: bfloat16 [3072, 5376], P('tp'), may hold values from -0.25 to 0.25
- gain_input: float32 [5376], replicated, may hold values from 0.5 to 1.5
- gain_query: float32 [128], replicated, may hold values from 0.5 to 1.5
- gain_key: float32 [128], replicated, may hold values from 0.5 to 1.5
- gain_post: float32 [5376], replicated, may hold values from 0.5 to 1.5
- gain_pre: float32 [5376], replicated, may hold values from 0.5 to 1.5
Outputs:
- hidden: bfloat16 [12288, 5376], P('seq', 'tp')
- ffn_input: bfloat16 [12288, 5376], P('seq', 'tp')
Inputs may be any that keep to these rules, and one draw needn't show every extreme that they name: positions[0] is 0, and every later entry is either 0 (a document starts there) or the entry before it plus 1; no document is longer than 2048 tokens.
All inputs are finite; a program needn't handle non-finite values.
Results may differ from a plain program's by a relative error of at most 0.0096.
Values may be sent and summed in bfloat16 or wider, within the bound.
A program may use at most 128 MiB of HBM per device.

v0:
```python
import jax
import jax.numpy as jnp
from jax import lax
from jax.sharding import Mesh
from jax.sharding import PartitionSpec as P

HEAD_DIM = 128
WINDOW = 1024
TP = ("tp_0", "tp_1")


norm_eps = 1e-06
query_scale = 168.0 ** (-0.5)
rope_base = 10000.0


def shifted(value, axis, steps):
    count = lax.axis_size(axis)
    leading, last = (max(0, -steps), min(count, count - steps))
    return lax.ppermute(value, axis, [(source, source + steps) for source in range(leading, last)])


def by_axis(shard, axes):
    for axis in axes:
        shard = lax.psum(shard, axis)
    return shard


def copy_for_each(shard, axis):
    devices = lax.axis_size(axis)
    return lax.all_to_all(
        jnp.broadcast_to(shard[None], (devices, *shard.shape)), axis, 0, 0, tiled=True
    )


def of_everyone(shard, axis):
    return copy_for_each(shard, axis).sum(axis=0)


def rms_scale(field, weight_gain):
    square_mean = jnp.mean(field * field, axis=-1, keepdims=True)
    return field * lax.rsqrt(square_mean + norm_eps) * weight_gain


def rotate(field, positions):
    half_dim = field.shape[-1] // 2
    inverse_freq = jnp.exp(-jnp.log(rope_base) * jnp.arange(half_dim, dtype=jnp.float32) / half_dim)
    angles = positions.astype(jnp.float32)[:, None] * inverse_freq[None, :]
    cosine = jnp.cos(angles)[:, None, :]
    sine = jnp.sin(angles)[:, None, :]
    first_half = field[..., :half_dim]
    second_half = field[..., half_dim:]
    return jnp.concatenate(
        [first_half * cosine - second_half * sine, second_half * cosine + first_half * sine],
        axis=-1,
    )


def head_project(normed, weight, weight_gain, positions):
    projected = jnp.dot(normed, weight, preferred_element_type=jnp.float32)
    projected = projected.reshape(normed.shape[0], -1, HEAD_DIM)
    return rotate(rms_scale(projected, weight_gain), positions).astype(jnp.bfloat16)


def local(
    tokens,
    positions,
    w_query,
    w_key,
    w_value,
    w_out,
    gain_input,
    gain_query,
    gain_key,
    gain_post,
    gain_pre,
):
    tok_rows = tokens.shape[0]
    gathered = lax.all_gather(tokens, TP, axis=1, tiled=True)
    width = gathered.shape[1]
    normed = rms_scale(gathered.astype(jnp.float32), gain_input).astype(jnp.bfloat16)
    query_rows = head_project(normed, w_query, gain_query, positions)
    key_rows = head_project(normed, w_key, gain_key, positions)
    value_rows = jnp.dot(normed, w_value, preferred_element_type=jnp.float32).astype(jnp.bfloat16)
    query_heads = query_rows.shape[1]
    key_heads = key_rows.shape[1]
    key_pair = (key_rows.reshape(tok_rows, key_heads * HEAD_DIM), value_rows)
    reach_blocks = (WINDOW + tok_rows - 2) // tok_rows
    blocks = []
    for shard_back in range(reach_blocks, 0, -1):
        blocks.append(shifted((key_pair[0], key_pair[1]), "seq", shard_back))
    blocks.append(key_pair)
    key_count = (reach_blocks + 1) * tok_rows
    key_all = jnp.concatenate([pair[0] for pair in blocks], axis=0).reshape(
        key_count, key_heads, HEAD_DIM
    )
    value_all = jnp.concatenate([pair[1] for pair in blocks], axis=0).reshape(
        key_count, key_heads, HEAD_DIM
    )
    first_row = lax.axis_index("seq") * tok_rows
    query_index = first_row + jnp.arange(tok_rows, dtype=jnp.int32)
    key_index = first_row - reach_blocks * tok_rows + jnp.arange(key_count, dtype=jnp.int32)
    doc_start = query_index - positions
    visible = (
        (key_index[None, :] >= doc_start[:, None])
        & (key_index[None, :] > query_index[:, None] - WINDOW)
        & (key_index[None, :] <= query_index[:, None])
    )
    query_groups = query_rows.reshape(tok_rows, key_heads, query_heads // key_heads, HEAD_DIM)
    scores = (
        jnp.einsum("tkgd,skd->kgts", query_groups, key_all, preferred_element_type=jnp.float32)
        * query_scale
    )
    weights = jnp.where(visible[None, None], jnp.exp(scores), 0.0)
    totals = jnp.sum(weights, axis=-1)
    numer = jnp.einsum(
        "kgts,skd->tkgd",
        weights.astype(jnp.bfloat16),
        value_all,
        preferred_element_type=jnp.float32,
    )
    attended = (numer / jnp.transpose(totals, (2, 0, 1))[..., None]).astype(jnp.bfloat16)
    attended = attended.reshape(tok_rows, query_heads * HEAD_DIM)
    partial_sum = jnp.dot(attended, w_out, preferred_element_type=jnp.float32)
    col_count = width // lax.axis_size(TP)
    col_start = lax.axis_index(TP) * col_count
    own_sum = lax.psum_scatter(
        partial_sum.astype(jnp.bfloat16), TP, scatter_dimension=1, tiled=True
    ).astype(jnp.float32)
    squares = by_axis(jnp.sum(own_sum * own_sum, axis=-1), TP)
    post_gain = lax.dynamic_slice_in_dim(gain_post, col_start, col_count, 0)
    post_part = own_sum * lax.rsqrt(squares / width + norm_eps)[:, None] * post_gain
    hidden_own = (tokens.astype(jnp.float32) + post_part).astype(jnp.bfloat16)
    hidden_wide = hidden_own.astype(jnp.float32)
    squares_next = of_everyone(jnp.sum(hidden_wide * hidden_wide, axis=-1), TP)
    pre_gain = lax.dynamic_slice_in_dim(gain_pre, col_start, col_count, 0)
    ffn_own = (hidden_wide * lax.rsqrt(squares_next / width + norm_eps)[:, None] * pre_gain).astype(
        jnp.bfloat16
    )
    return (hidden_own, ffn_own)


def solution(mesh):
    torus = Mesh(mesh.devices.reshape(mesh.shape["seq"], 2, 2), ("seq", "tp_0", "tp_1"))
    return jax.shard_map(
        local,
        mesh=torus,
        in_specs=(
            P("seq", TP),
            P("seq"),
            P(None, TP),
            P(None, TP),
            P(None, TP),
            P(TP, None),
            P(),
            P(),
            P(),
            P(),
            P(),
        ),
        out_specs=(P("seq", TP), P("seq", TP)),
        check_vma=False,
    )
```

profile of v0, /device:TPU:65, one launch (start us, length us, event | category | flops | bytes accessed | tf_op | source)
XLA Modules:
  0.0 202.8 jit_solution(1063424080448496862)
XLA Ops:
  10.1 47.4 %all-gather.2.cloned.1.call-done = bf16[384,5376]{0,1:T(8,128)(2,1)} async-done(((bf16[384,1344]{0,1:T(8,128)(2,1)}), bf16[384,5376]{0,1:T(8,128)(2,1)}) %all-gather.2.cloned.1.call-update) | async-done | bytes 4128784 | tf_op jit(solution)/shard_map/all_gather | solution.py:79
  57.5 3.3 %fusion.2 = f32[384]{0:T(512)S(1)} fusion(bf16[384,5376]{0,1:T(8,128)(2,1)} %all-gather.2.cloned.1.call-done), kind=kLoop, calls=%fused_computation.6 | loop fusion | flops 6192768 | bytes 4130304 | tf_op jit(solution)/shard_map/reduce_sum | solution.py:41
  61.0 5.7 %convolution_convert_fusion.1 = bf16[384,384]{1,0:T(8,128)(2,1)S(1)} fusion(bf16[5376,384]{1,0:T(8,128)(2,1)} %param.15, bf16[384,5376]{0,1:T(8,128)(2,1)S(1)} %copy-done.1, f32[5376]{0:T(1024)S(1)} %copy-done.10, f32[384]{0:T(512)S(1)} %add_rsqrt_fusion.4), kind=kOutput, calls=%fused_computation.26 | convolution fusion | flops 1593851904 | bytes 8575488 | tf_op jit(solution)/shard_map/dot_general | solution.py:84
  66.7 3.2 %collective-permute-start.2 = (bf16[384,384]{1,0:T(8,128)(2,1)S(1)}, bf16[384,384]{1,0:T(8,128)(2,1)S(1)}, u32[]{:S(2)}, u32[]{:S(2)}) collective-permute-start(bf16[384,384]{1,0:T(8,128)(2,1)S(1)} %convolution_convert_fusion.1), channel_id=1, source_target_pairs={{0,4},{4,8},{8,12},{12,16},{16,20},{20,24},{24,28},{28,32},{32,36}... | collective-permute-start | bytes 884744 | tf_op jit(solution)/shard_map/ppermute | solution.py:20
  70.0 4.3 %collective-permute-start.1 = (bf16[384,384]{1,0:T(8,128)(2,1)S(1)}, bf16[384,384]{1,0:T(8,128)(2,1)S(1)}, u32[]{:S(2)}, u32[]{:S(2)}) collective-permute-start(bf16[384,384]{1,0:T(8,128)(2,1)S(1)} %convolution_convert_fusion.1), channel_id=1, source_target_pairs={{0,8},{4,12},{8,16},{12,20},{16,24},{20,28},{24,32},{28,36},{32,40... | collective-permute-start | bytes 884744 | tf_op jit(solution)/shard_map/ppermute | solution.py:20
  74.3 4.0 %collective-permute-start = (bf16[384,384]{1,0:T(8,128)(2,1)S(1)}, bf16[384,384]{1,0:T(8,128)(2,1)}, u32[]{:S(2)}, u32[]{:S(2)}) collective-permute-start(bf16[384,384]{1,0:T(8,128)(2,1)S(1)} %convolution_convert_fusion.1), channel_id=1, source_target_pairs={{0,12},{4,16},{8,20},{12,24},{16,28},{20,32},{24,36},{28,40},{32,4... | collective-permute-start | bytes 884744 | tf_op jit(solution)/shard_map/ppermute | solution.py:20
  78.3 2.8 %fusion.39 = f32[384,384]{0,1:T(8,128)S(1)} fusion(bf16[5376,384]{1,0:T(8,128)(2,1)S(1)} %copy-done.9, bf16[384,5376]{0,1:T(8,128)(2,1)S(1)} %copy-done.1, f32[5376]{0:T(1024)S(1)} %copy-done.10, f32[384]{0:T(512)S(1)} %add_rsqrt_fusion.4), kind=kOutput, calls=%fused_computation.65 | convolution fusion | flops 1593704448 | bytes 8870400 | tf_op jit(solution)/shard_map/dot_general | solution.py:60
  82.1 0.9 copy.59
  83.0 2.3 %collective-permute-start.5 = (bf16[384,384]{0,1:T(8,128)(2,1)}, bf16[384,384]{0,1:T(8,128)(2,1)}, u32[]{:S(2)}, u32[]{:S(2)}) collective-permute-start(bf16[384,384]{0,1:T(8,128)(2,1)} %bitcast.4), channel_id=1, source_target_pairs={{0,4},{4,8},{8,12},{12,16},{16,20},{20,24},{24,28},{28,32},{32,36}... | collective-permute-start | bytes 884744 | tf_op jit(solution)/shard_map/ppermute | solution.py:20
  85.3 3.6 %collective-permute-start.4 = (bf16[384,384]{0,1:T(8,128)(2,1)}, bf16[384,384]{0,1:T(8,128)(2,1)}, u32[]{:S(2)}, u32[]{:S(2)}) collective-permute-start(bf16[384,384]{0,1:T(8,128)(2,1)} %bitcast.4), channel_id=1, source_target_pairs={{0,8},{4,12},{8,16},{12,20},{16,24},{20,28},{24,32},{28,36},{32,40... | collective-permute-start | bytes 884744 | tf_op jit(solution)/shard_map/ppermute | solution.py:20
  88.9 9.3 %fusion.37 = f32[384,768]{0,1:T(8,128)S(1)} fusion(bf16[5376,768]{1,0:T(8,128)(2,1)} %param.13, bf16[384,5376]{0,1:T(8,128)(2,1)} %all-gather.2.cloned.1.call-done, f32[5376]{0:T(1024)S(1)} %copy-done.10, f32[384]{0:T(512)S(1)} %add_rsqrt_fusion.4), kind=kOutput, calls=%fused_computation.64 | convolution fusion | flops 3179151360 | bytes 13588992 | tf_op jit(solution)/shard_map/dot_general | solution.py:60
  98.5 4.0 %collective-permute-start.3 = (bf16[384,384]{0,1:T(8,128)(2,1)}, bf16[384,384]{0,1:T(8,128)(2,1)}, u32[]{:S(2)}, u32[]{:S(2)}) collective-permute-start(bf16[384,384]{0,1:T(8,128)(2,1)} %bitcast.4), channel_id=1, source_target_pairs={{0,12},{4,16},{8,20},{12,24},{16,28},{20,32},{24,36},{28,40},{32,4... | collective-permute-start | bytes 884744 | tf_op jit(solution)/shard_map/ppermute | solution.py:20
  102.7 1.1 copy.65
  103.8 1.1 copy.64
  105.6 1.3 pad_maximum_fusion
  106.9 0.9 copy.55
  107.8 1.2 copy.62
  109.0 1.2 copy.61
  110.1 3.7 %collective-permute-done.3 = bf16[384,384]{0,1:T(8,128)(2,1)} collective-permute-done((bf16[384,384]{0,1:T(8,128)(2,1)}, bf16[384,384]{0,1:T(8,128)(2,1)}, u32[]{:S(2)}, u32[]{:S(2)}) %collective-permute-start.3) | collective-permute-done | bytes 294944 | tf_op jit(solution)/shard_map/ppermute | solution.py:20
  113.8 1.2 copy.60
  115.0 5.2 %fusion = (f32[3,2,384]{2,1,0:T(2,128)S(1)}, f32[3,1536,384,2]{2,1,3,0:T(8,128)S(1)}) fusion(pred[384,1536]{0,1:T(8,128)(4,1)S(1)} %compare_and_fusion, bf16[384,3,2,64]{3,0,2,1:T(8,128)(2,1)} %bitcast.48, bf16[384,3,2,64]{3,0,2,1:T(8,128)(2,1)} %bitcast.49, bf16[384,3,128]{2,0,1:T(8,128)(2,1)S(1)} %maximum_convert_fusion, ...), kind=kOutput, calls=%fused_computation.1 | convolution fusion | flops 922482432 | bytes 16524288 | tf_op jit(solution)/shard_map/tkgd,skd->kgts/dot_general | solution.py:111
  120.2 3.0 %divide_convert_fusion = bf16[384,3,2,128]{0,3,2,1:T(8,128)(2,1)S(1)} fusion(bf16[1536,3,128,1]{0,2,3,1:T(8,128)(2,1)S(1)} %bitcast.47, f32[3,1536,384,2]{2,1,3,0:T(8,128)S(1)} %get-tuple-element.13, pred[384,1536]{0,1:T(8,128)(4,1)S(1)} %compare_and_fusion, f32[384,3,2]{0,2,1:T(2,128)S(1)} %bitcast.51), kind=kOutput, calls=%fused_computation.36 | convolution fusion | flops 917176320 | bytes 16524288 | tf_op jit(solution)/shard_map/kgts,skd->tkgd/dot_general | solution.py:116
  123.2 9.7 %convolution_convert_fusion = bf16[384,5376]{0,1:T(8,128)(2,1)} fusion(bf16[384,768]{0,1:T(8,128)(2,1)S(1)} %bitcast.50, bf16[768,5376]{1,0:T(8,128)(2,1)} %param.16), kind=kOutput, calls=%fused_computation.5 | convolution fusion | flops 3172958208 | bytes 12976128 | tf_op jit(solution)/shard_map/dot_general | solution.py:124
  132.9 0.9 dynamic_slice.6
  133.8 42.9 %reduce-scatter.2.cloned.1.call-done = bf16[384,1344]{0,1:T(8,128)(2,1)} async-done(((bf16[384,5376]{0,1:T(8,128)(2,1)}), bf16[384,1344]{0,1:T(8,128)(2,1)}) %reduce-scatter.2.cloned.1.call-update) | async-done | bytes 1032208 | tf_op jit(solution)/shard_map/reduce_scatter | solution.py:127
  176.7 1.5 fusion.10
  178.2 3.8 %psum.14 = f32[384]{0:T(512)S(1)} all-reduce(f32[384]{0:T(512)S(1)} %fusion.10), channel_id=1, replica_groups=mesh['seq'=32,'tp_0'=2,'tp_1'=2] {'tp_0'}, use_global_device_ids=true, to_apply=%region_6.7 | all-reduce | flops 384 | bytes 3072 | tf_op jit(solution)/shard_map/psum | solution.py:25
  182.0 3.6 %psum.15 = f32[384]{0:T(512)S(1)} all-reduce(f32[384]{0:T(512)S(1)} %psum.14), channel_id=1, replica_groups=mesh['seq'=32,'tp_0'=2,'tp_1'=2] {'tp_1'}, use_global_device_ids=true, to_apply=%region_7.8 | all-reduce | flops 384 | bytes 3072 | tf_op jit(solution)/shard_map/psum | solution.py:25
  185.6 1.8 fusion.14
  188.0 3.6 %all-to-all-start = ((f32[4,1,384]{2,1,0:T(1,128)}), f32[4,1,384]{2,1,0:T(1,128)S(1)}, u32[]{:S(2)}, u32[]{:S(2)}) async-start(f32[4,1,384]{2,1,0:T(1,128)} %broadcast_in_dim.12), calls=%async_computation.1 | async-start | bytes 12288 | tf_op jit(solution)/shard_map/all_to_all | solution.py:31
  192.4 2.3 %all-to-all-done = f32[4,1,384]{2,1,0:T(1,128)S(1)} async-done(((f32[4,1,384]{2,1,0:T(1,128)}), f32[4,1,384]{2,1,0:T(1,128)S(1)}, u32[]{:S(2)}, u32[]{:S(2)}) %all-to-all-start) | async-done | bytes 6176 | tf_op jit(solution)/shard_map/all_to_all | solution.py:31
  194.7 1.3 fusion.16
  (55 shorter events, 6.7 us)
Async XLA Ops:
  7.2 53.7 %copy-start.10 = (f32[5376]{0:T(1024)S(1)}, f32[5376]{0:T(1024)}, u32[]{:S(2)}) copy-start(f32[5376]{0:T(1024)} %param.17) | copy-start | bytes 64516
  7.2 50.4 %all-gather.2.cloned.1.call-start = ((), (), s32[]{:S(2)}) async-start(), calls=%async_computation.2 | async-start | bytes 5160960 | tf_op jit(solution)/shard_map/all_gather | solution.py:79
  7.9 168.8 %reduce-scatter.2.cloned.1.call-start = ((), (), s32[]{:S(2)}) async-start(), calls=%async_computation.3 | async-start | bytes 5160960 | tf_op jit(solution)/shard_map/reduce_scatter | solution.py:127
  57.5 3.4 %copy-start.1 = (bf16[384,5376]{0,1:T(8,128)(2,1)S(1)}, bf16[384,5376]{0,1:T(8,128)(2,1)}, u32[]{:S(2)}) copy-start(bf16[384,5376]{0,1:T(8,128)(2,1)} %all-gather.2.cloned.1.call-done) | copy-start | bytes 12386308
  61.0 17.3 %copy-start.9 = (bf16[5376,384]{1,0:T(8,128)(2,1)S(1)}, bf16[5376,384]{1,0:T(8,128)(2,1)}, u32[]{:S(2)}) copy-start(bf16[5376,384]{1,0:T(8,128)(2,1)} %param.14) | copy-start | bytes 12386308
  66.7 14.4 %copy-start.3 = (bf16[384,384]{1,0:T(8,128)(2,1)}, bf16[384,384]{1,0:T(8,128)(2,1)S(1)}, u32[]{:S(2)}) copy-start(bf16[384,384]{1,0:T(8,128)(2,1)S(1)} %convolution_convert_fusion.1) | copy-start | bytes 884740
  66.7 14.7 %copy-start.7 = (f32[128]{0:T(128)S(1)}, f32[128]{0:T(128)}, u32[]{:S(2)}) copy-start(f32[128]{0:T(128)} %param.19) | copy-start | bytes 1540
  66.7 31.8 %collective-permute-start.2 = (bf16[384,384]{1,0:T(8,128)(2,1)S(1)}, bf16[384,384]{1,0:T(8,128)(2,1)S(1)}, u32[]{:S(2)}, u32[]{:S(2)}) collective-permute-start(bf16[384,384]{1,0:T(8,128)(2,1)S(1)} %convolution_convert_fusion.1), channel_id=1, source_target_pairs={{0,4},{4,8},{8,12},{12,16},{16,20},{20,24},{24,28},{28,32},{32,36}... | collective-permute-start | bytes 884744 | tf_op jit(solution)/shard_map/ppermute | solution.py:20
  70.0 34.9 %collective-permute-start.1 = (bf16[384,384]{1,0:T(8,128)(2,1)S(1)}, bf16[384,384]{1,0:T(8,128)(2,1)S(1)}, u32[]{:S(2)}, u32[]{:S(2)}) collective-permute-start(bf16[384,384]{1,0:T(8,128)(2,1)S(1)} %convolution_convert_fusion.1), channel_id=1, source_target_pairs={{0,8},{4,12},{8,16},{12,20},{16,24},{20,28},{24,32},{28,36},{32,40... | collective-permute-start | bytes 884744 | tf_op jit(solution)/shard_map/ppermute | solution.py:20
  74.3 31.3 %collective-permute-start = (bf16[384,384]{1,0:T(8,128)(2,1)S(1)}, bf16[384,384]{1,0:T(8,128)(2,1)}, u32[]{:S(2)}, u32[]{:S(2)}) collective-permute-start(bf16[384,384]{1,0:T(8,128)(2,1)S(1)} %convolution_convert_fusion.1), channel_id=1, source_target_pairs={{0,12},{4,16},{8,20},{12,24},{16,28},{20,32},{24,36},{28,40},{32,4... | collective-permute-start | bytes 884744 | tf_op jit(solution)/shard_map/ppermute | solution.py:20
  83.0 15.3 %copy-start.8 = (f32[128]{0:T(128)S(1)}, f32[128]{0:T(128)}, u32[]{:S(2)}) copy-start(f32[128]{0:T(128)} %param.18) | copy-start | bytes 1540
  83.0 24.8 %collective-permute-start.5 = (bf16[384,384]{0,1:T(8,128)(2,1)}, bf16[384,384]{0,1:T(8,128)(2,1)}, u32[]{:S(2)}, u32[]{:S(2)}) collective-permute-start(bf16[384,384]{0,1:T(8,128)(2,1)} %bitcast.4), channel_id=1, source_target_pairs={{0,4},{4,8},{8,12},{12,16},{16,20},{20,24},{24,28},{28,32},{32,36}... | collective-permute-start | bytes 884744 | tf_op jit(solution)/shard_map/ppermute | solution.py:20
  85.3 23.6 %collective-permute-start.4 = (bf16[384,384]{0,1:T(8,128)(2,1)}, bf16[384,384]{0,1:T(8,128)(2,1)}, u32[]{:S(2)}, u32[]{:S(2)}) collective-permute-start(bf16[384,384]{0,1:T(8,128)(2,1)} %bitcast.4), channel_id=1, source_target_pairs={{0,8},{4,12},{8,16},{12,20},{16,24},{20,28},{24,32},{28,36},{32,40... | collective-permute-start | bytes 884744 | tf_op jit(solution)/shard_map/ppermute | solution.py:20
  98.2 7.4 %copy-start.4 = (bf16[384,384]{1,0:T(8,128)(2,1)S(1)}, bf16[384,384]{1,0:T(8,128)(2,1)}, u32[]{:S(2)}) copy-start(bf16[384,384]{1,0:T(8,128)(2,1)} %copy-done.3) | copy-start | bytes 884740
  98.5 6.3 %copy-start.5 = (bf16[384,384]{1,0:T(8,128)(2,1)}, bf16[384,384]{1,0:T(8,128)(2,1)S(1)}, u32[]{:S(2)}) copy-start(bf16[384,384]{1,0:T(8,128)(2,1)S(1)} %collective-permute-done.2) | copy-start | bytes 884740
  98.5 15.3 %collective-permute-start.3 = (bf16[384,384]{0,1:T(8,128)(2,1)}, bf16[384,384]{0,1:T(8,128)(2,1)}, u32[]{:S(2)}, u32[]{:S(2)}) collective-permute-start(bf16[384,384]{0,1:T(8,128)(2,1)} %bitcast.4), channel_id=1, source_target_pairs={{0,12},{4,16},{8,20},{12,24},{16,28},{20,32},{24,36},{28,40},{32,4... | collective-permute-start | bytes 884744 | tf_op jit(solution)/shard_map/ppermute | solution.py:20
  104.9 0.7 copy-start.6
  132.9 52.7 %copy-start.2 = (bf16[384,1344]{0,1:T(8,128)(2,1)S(1)}, bf16[384,1344]{0,1:T(8,128)(2,1)}, u32[]{:S(2)}) copy-start(bf16[384,1344]{0,1:T(8,128)(2,1)} %param.11) | copy-start | bytes 3096580
  187.4 8.6 %copy-start = (bf16[384,1344]{0,1:T(8,128)(2,1)}, bf16[384,1344]{0,1:T(8,128)(2,1)S(1)}, u32[]{:S(2)}) copy-start(bf16[384,1344]{0,1:T(8,128)(2,1)S(1)} %get-tuple-element.3) | copy-start | bytes 3096580
  188.0 6.7 %all-to-all-start = ((f32[4,1,384]{2,1,0:T(1,128)}), f32[4,1,384]{2,1,0:T(1,128)S(1)}, u32[]{:S(2)}, u32[]{:S(2)}) async-start(f32[4,1,384]{2,1,0:T(1,128)} %broadcast_in_dim.12), calls=%async_computation.1 | async-start | bytes 12288 | tf_op jit(solution)/shard_map/all_to_all | solution.py:31
Sparse Core Ops, SparseCore 0:
  9.7 47.8 all-gather.1
  133.0 43.5 reduce-scatter.1
where the time goes:
time: 205 us; the launch traced here: 203 us
  waiting for transfers between devices  97 us (47%)
  matrix products  35.7 us (17%)
  starting transfers between devices  25.1 us (12%)
  between operations  14.4 us (7%)
  other arithmetic  12.2 us (6%)
  local copies, waits for them, and re-layouts  11 us (5%)
  blocking collectives  7.43 us (4%)
    all_gather x1, waiting for transfers between devices, local(): gathered = lax.all_gather(tokens, TP, axis=1, tiled=True)  47.4 us
    reduce_scatter x1, waiting for transfers between devices, local(): lax.psum_scatter(partial_sum.astype(jnp.bfloat16), TP, scatter_dimension=...  42.9 us
    ppermute x6, starting transfers between devices, shifted(): lax.ppermute(value, axis, [(source, source + steps) for source in range(l...  21.5 us
    dot_general x2, matrix products, head_project(): projected = jnp.dot(normed, weight, preferred_element_type=jnp.float32)  12.1 us
    dot_general x1, matrix products, local(): partial_sum = jnp.dot(attended, w_out, preferred_element_type=jnp.float32)  9.74 us
    psum x2, blocking collectives, by_axis(): shard = lax.psum(shard, axis)  7.43 us
    dot_general x1, matrix products, local(): jnp.dot(normed, w_value, preferred_element_type=jnp.float32)  5.74 us
    dot_general x1, matrix products, local(): jnp.einsum('tkgd,skd->kgts', query_groups, key_all, preferred_element_typ...  5.18 us
  transfers between devices with their start and end apart: 9, of which 5 were waited for; matrix products, arithmetic and copies ran while one was open for 12% of the time, Pallas kernels for 0%

commit v1 on v0

v1 whole, which is shorter than its diff:
```python
import functools
import math

import jax
import jax.numpy as jnp
from jax import lax
from jax.experimental import pallas as pl
from jax.experimental.pallas import tpu as pltpu
from jax.sharding import Mesh
from jax.sharding import PartitionSpec as P

F32 = jnp.float32
BF16 = jnp.bfloat16
MESH = pl.DeviceIdType.MESH

EPS = 1e-6
WIDTH = 5376
OWN = 1344
HALF = 672
PAD = 1408
ROWS = 384
CH = 128
NC = 3
KV = 768
N_SEQ = 32
SCORE = 168.0**-0.5 * math.log2(math.e)


def kernel(
    xt, pos, wq, wk, wv, wo, gi, gq, gk, gpost, gpre,
    hid, ffn,
    xg, wqv, wkv, wvv, wov, acc, ss, gtab, rope_c, rope_s, bias,
    qs, kvb, o_acc, l_acc, att, rs_send, rs_recv, own, tok, st_send, st_recv,
    s_own, s_sib, r_sib, s_z, r_z, s_f, r_f, s_w, s_wo, s_wos, r_wos,
    s_kv, r_kv, s_at, r_at, s_rs, r_rs, s_st, r_st,
):
    seq = lax.axis_index("seq")
    zl = lax.axis_index("tp_0")
    core = lax.axis_index("tp_1")

    def peer(k):
        return (seq, lax.rem(zl + k // 2, 2), lax.rem(core + k % 2, 2))

    def tp_of(k):
        return lax.rem(zl + k // 2, 2) * 2 + lax.rem(core + k % 2, 2)

    def col_start(k):
        t = tp_of(k)
        return pl.multiple_of(OWN * t - 64 * lax.rem(t, 2), 128)

    def later(k):
        return (lax.rem(seq + k, N_SEQ), zl, core)

    barrier = pltpu.get_barrier_semaphore()
    for k in (1, 2, 3):
        pl.semaphore_signal(barrier, inc=1, device_id=peer(k), device_id_type=MESH)
        pl.semaphore_signal(barrier, inc=1, device_id=later(k), device_id_type=MESH)
        pl.semaphore_signal(barrier, inc=1, device_id=later(N_SEQ - k), device_id_type=MESH)
    pl.semaphore_wait(barrier, 9)

    def remote(src, dst, ss_, rs_, dev):
        return pltpu.make_async_remote_copy(
            src_ref=src, dst_ref=dst, send_sem=ss_, recv_sem=rs_, device_id=dev, device_id_type=MESH
        )

    def piece(ref, c, h):
        return ref.at[pl.ds(h * HALF, HALF), pl.ds(c * CH, CH)]

    def z_copy(c, h):
        return remote(piece(xt, c, h), piece(xg.at[2], c, h), s_z.at[c, h], r_z.at[c, h], peer(2))

    def f_copy(c, h):
        return remote(piece(xg.at[2], c, h), piece(xg.at[3], c, h), s_f.at[c, h], r_f.at[c, h], peer(1))

    sib_copy = remote(xt, xg.at[1], s_sib, r_sib, peer(1))
    own_copy = pltpu.make_async_copy(xt, xg.at[0], s_own)

    def w_copies(k):
        first = pl.multiple_of(tp_of(k) * OWN, 16)
        return [
            pltpu.make_async_copy(a.at[pl.ds(first, OWN)], b.at[k], s_w.at[i, k])
            for i, (a, b) in enumerate(((wq, wqv), (wk, wkv), (wv, wvv)))
        ]

    wo_copies = [
        pltpu.make_async_copy(wo.at[:, pl.ds(col_start(k), PAD)], wov.at[i, pl.ds(0, KV)], s_wo.at[i])
        for i, k in enumerate((2, 0))
    ]
    wo_remote = [
        remote(wo.at[:, pl.ds(col_start(k), PAD)], wov.at[i, pl.ds(KV, KV)], s_wos.at[i], r_wos.at[i], peer(1))
        for i, k in enumerate((3, 1))
    ]

    def kv_copy(k, c):
        return remote(
            kvb.at[c, pl.ds(3 * CH, CH)],
            kvb.at[c, pl.ds((3 - k) * CH, CH)],
            s_kv.at[k - 1, c],
            r_kv.at[k - 1, c],
            later(k),
        )

    def att_copy(c):
        return remote(
            att.at[pl.ds(c * CH, CH), pl.ds(0, KV)],
            att.at[pl.ds(c * CH, CH), pl.ds(KV, KV)],
            s_at.at[c],
            r_at.at[c],
            peer(1),
        )

    def rs_copy(c):
        return remote(rs_send.at[c], rs_recv.at[c], s_rs.at[c], r_rs.at[c], peer(2))

    def st_copy(c, k):
        return remote(st_send.at[c], st_recv.at[c, k - 1], s_st.at[c, k - 1], r_st.at[c, k - 1], peer(k))

    for c in range(NC):
        for h in range(2):
            z_copy(c, h).start()
    own_copy.start()
    sib_copy.start()
    for k in range(4):
        for cp in w_copies(k):
            cp.start()
    for cp in wo_copies + wo_remote:
        cp.start()

    acc[...] = jnp.zeros_like(acc)
    ss[...] = jnp.zeros_like(ss)
    o_acc[...] = jnp.zeros_like(o_acc)
    l_acc[...] = jnp.zeros_like(l_acc)
    for k in (1, 2, 3):
        @pl.when(seq < k)
        def _():
            for c in range(NC):
                kvb[c, pl.ds((3 - k) * CH, CH), :] = jnp.zeros((CH, KV), BF16)
    kvb[0, pl.ds(0, CH), :] = jnp.zeros((CH, KV), BF16)

    for i in range(8):
        gtab[i] = jnp.broadcast_to(gi[:, pl.ds(i * HALF, HALF)], (8, HALF))

    lane = lax.broadcasted_iota(jnp.int32, (CH, CH), 1)
    sub = lax.broadcasted_iota(jnp.int32, (CH, CH), 0)
    half_lane = jnp.where(lane >= 64, lane - 64, lane).astype(F32)
    inverse_freq = jnp.exp(half_lane * (-math.log(10000.0) / 64))
    for c in range(NC):
        p_row = pos[:, pl.ds(c * CH, CH)].astype(F32)
        p_mat = jnp.broadcast_to(p_row, (CH, CH)).T
        angle = p_mat * inverse_freq
        sine = jnp.sin(angle)
        rope_c[c] = jnp.cos(angle)
        rope_s[c] = jnp.where(lane < 64, -sine, sine)
        i_rel = sub + c * CH
        low = i_rel - jnp.minimum(p_mat.astype(jnp.int32), 1023)
        for cc in range(NC):
            first = 3 if cc > c else 2
            for n in range(3):
                j_rel = CH * cc + ROWS * (n - first) + lane
                bias[c, cc, :, pl.ds(n * CH, CH)] = jnp.where((j_rel >= low) & (j_rel <= i_rel), 0.0, -1e30)

    own_copy.wait()
    for c in range(NC):
        x = xg[0, :, pl.ds(c * CH, CH)].astype(F32).T
        x = jnp.concatenate([x, jnp.zeros((CH, PAD - OWN), F32)], axis=1)
        tok[pl.ds(c * CH, CH), :] = jnp.where(core == 1, pltpu.roll(x, 64, 1), x)

    def step(k, c, h):
        cols = pl.ds(pl.multiple_of(c * CH, CH), CH)
        feats = pl.ds(pl.multiple_of(h * HALF, 16), HALF)
        x = xg[k, feats, cols].astype(F32)
        ss[c] += jnp.broadcast_to(jnp.sum(x * x, axis=0, keepdims=True), (8, CH))
        gain = gtab[tp_of(k) * 2 + h, pl.ds(0, 1), :]
        x = (x.T * gain).astype(BF16)
        acc[cols, pl.ds(0, 768)] += jnp.dot(x, wqv[k, feats, :], preferred_element_type=F32)
        acc[cols, pl.ds(768, 384)] += jnp.dot(x, wkv[k, feats, :], preferred_element_type=F32)
        acc[cols, pl.ds(1152, 384)] += jnp.dot(x, wvv[k, feats, :], preferred_element_type=F32)

    def local_steps(k):
        for cp in w_copies(k):
            cp.wait()

        @pl.loop(0, NC * 2)
        def _(i):
            step(k, i // 2, lax.rem(i, 2))

    local_steps(0)
    sib_copy.wait_recv()
    local_steps(1)
    for k in (2, 3):
        for cp in w_copies(k):
            cp.wait()

    def head(u, gain, c):
        mean = jnp.mean(u * u, axis=-1, keepdims=True)
        u = u * lax.rsqrt(mean + EPS) * gain
        return (u * rope_c[c] + pltpu.roll(u, 64, 1) * rope_s[c]).astype(BF16)

    def finish(c):
        rows = pl.ds(c * CH, CH)
        mean = ss[c, pl.ds(0, 1), :] / WIDTH
        scale = jnp.broadcast_to(lax.rsqrt(mean + EPS), (CH, CH)).T
        for h in range(3):
            u = acc[rows, pl.ds(768 + h * 128, 128)] * scale
            kvb[c, pl.ds(3 * CH, CH), pl.ds(h * 128, 128)] = head(u, gk[...], c)
            v = acc[rows, pl.ds(1152 + h * 128, 128)] * scale
            kvb[c, pl.ds(3 * CH, CH), pl.ds(384 + h * 128, 128)] = v.astype(BF16)
        for k in (1, 2, 3):
            if k == 3 and c == 0:
                continue

            @pl.when(seq + k < N_SEQ)
            def _():
                kv_copy(k, c).start()
        for h in range(3):
            for g in range(2):
                u = acc[rows, pl.ds((2 * h + g) * 128, 128)] * scale
                qs[c, h, pl.ds(g * CH, CH), :] = head(u, gq[...], c)

    for c in range(NC):
        @pl.loop(0, 2)
        def _(h):
            z_copy(c, h).wait_recv()
            f_copy(c, h).start()
            step(2, c, h)
            f_copy(c, h).wait_recv()
            step(3, c, h)

        finish(c)

    def unit(c, cc):
        start = 0 if cc > c else CH
        b = bias[c, cc]
        b = jnp.concatenate([b, b], axis=0)
        for h in range(3):
            keys = kvb[cc, pl.ds(start, 3 * CH), pl.ds(h * 128, 128)]
            vals = kvb[cc, pl.ds(start, 3 * CH), pl.ds(384 + h * 128, 128)]
            s = lax.dot_general(qs[c, h], keys, (((1,), (1,)), ((), ())), preferred_element_type=F32)
            w = jnp.exp2(s * SCORE + b)
            l_acc[c, h] += w[:, 0:128] + w[:, 128:256] + w[:, 256:384]
            o_acc[c, h] += jnp.dot(w.astype(BF16), vals, preferred_element_type=F32)

    def kv_arrived(cc):
        for k in (1, 2, 3):
            if k == 3 and cc == 0:
                continue

            @pl.when(seq >= k)
            def _():
                kv_copy(k, cc).wait_recv()

    for cc in range(2):
        kv_arrived(cc)
        for c in range(NC):
            unit(c, cc)
    kv_arrived(2)
    for cp in wo_copies:
        cp.wait()
    for cp in wo_remote:
        cp.wait()

    def project(c, i):
        return jnp.dot(att[pl.ds(c * CH, CH), :], wov[i], preferred_element_type=F32)

    for c in range(NC):
        unit(c, 2)
        for h in range(3):
            total = jnp.sum(l_acc[c, h], axis=-1, keepdims=True)
            o = (o_acc[c, h] / total).astype(BF16)
            att[pl.ds(c * CH, CH), pl.ds(2 * h * 128, 128)] = o[:CH]
            att[pl.ds(c * CH, CH), pl.ds((2 * h + 1) * 128, 128)] = o[CH:]
        att_copy(c).start()
        if c > 0:
            att_copy(c - 1).wait_recv()
            rs_send[c - 1] = project(c - 1, 0).astype(BF16)
            rs_copy(c - 1).start()
    att_copy(2).wait_recv()
    rs_send[2] = project(2, 0).astype(BF16)
    rs_copy(2).start()

    for c in range(NC):
        own[pl.ds(c * CH, CH), :] = project(c, 1)

    gain_post = gpost[:, pl.ds(col_start(0), PAD)]
    gain_pre = gpre[:, pl.ds(col_start(0), PAD)]
    col = lax.broadcasted_iota(jnp.int32, (1, PAD), 1) - 64 * core
    inside = ((col >= 0) & (col < OWN)).astype(F32)

    def stats(c):
        rows = pl.ds(c * CH, CH)
        rs_copy(c).wait_recv()
        s = (own[rows, :] + rs_recv[c].astype(F32)) * inside
        own[rows, :] = s
        t = tok[rows, :]
        sg = s * gain_post
        both = [jnp.sum(v, axis=-1, keepdims=True) for v in (s * s, t * t, t * sg, sg * sg)]
        table = jnp.where(lane == 0, both[0], jnp.where(lane == 1, both[1], jnp.where(lane == 2, both[2], both[3])))
        st_send[c] = table.T[0:8, :]
        for k in (1, 2, 3):
            st_copy(c, k).start()

    def final(c):
        rows = pl.ds(c * CH, CH)
        for k in (1, 2, 3):
            st_copy(c, k).wait_recv()
        rows4 = st_send[c] + st_recv[c, 0] + st_recv[c, 1] + st_recv[c, 2]
        post = lax.rsqrt(rows4[0:1] / WIDTH + EPS)
        square = rows4[1:2] + 2.0 * post * rows4[2:3] + post * post * rows4[3:4]
        pre = lax.rsqrt(jnp.maximum(square, 0.0) / WIDTH + EPS)
        post = jnp.broadcast_to(post, (CH, CH)).T[:, 0:1]
        pre = jnp.broadcast_to(pre, (CH, CH)).T[:, 0:1]
        hidden = (tok[rows, :] + own[rows, :] * post * gain_post).astype(BF16).astype(F32)
        out = hidden * pre * gain_pre

        def place(v):
            return jnp.where(core == 1, pltpu.roll(v, PAD - 64, 1), v)[:, :OWN].astype(BF16)

        hid[rows, :] = place(hidden)
        ffn[rows, :] = place(out)

    for c in range(NC):
        stats(c)
        final(c)

    sib_copy.wait_send()
    for c in range(NC):
        for h in range(2):
            z_copy(c, h).wait_send()
            f_copy(c, h).wait_send()
        for k in (1, 2, 3):
            if not (k == 3 and c == 0):
                @pl.when(seq + k < N_SEQ)
                def _():
                    kv_copy(k, c).wait_send()
            st_copy(c, k).wait_send()
        att_copy(c).wait_send()
        rs_copy(c).wait_send()


def local(tokens, positions, w_query, w_key, w_value, w_out, gain_input, gain_query, gain_key, gain_post, gain_pre):
    hbm = pl.BlockSpec(memory_space=pltpu.MemorySpace.HBM)
    vmem = pl.BlockSpec(memory_space=pltpu.VMEM)
    dma = pltpu.SemaphoreType.DMA
    out = jax.ShapeDtypeStruct((ROWS, OWN), BF16)
    return pl.pallas_call(
        kernel,
        out_shape=(out, out),
        in_specs=[hbm, vmem, hbm, hbm, hbm, hbm, vmem, vmem, vmem, vmem, vmem],
        out_specs=(vmem, vmem),
        scratch_shapes=[
            pltpu.VMEM((4, OWN, ROWS), BF16),
            pltpu.VMEM((4, OWN, 768), BF16),
            pltpu.VMEM((4, OWN, 384), BF16),
            pltpu.VMEM((4, OWN, 384), BF16),
            pltpu.VMEM((2, 2 * KV, PAD), BF16),
            pltpu.VMEM((ROWS, 1536), F32),
            pltpu.VMEM((NC, 8, CH), F32),
            pltpu.VMEM((8, 8, HALF), F32),
            pltpu.VMEM((NC, CH, CH), F32),
            pltpu.VMEM((NC, CH, CH), F32),
            pltpu.VMEM((NC, NC, CH, 3 * CH), F32),
            pltpu.VMEM((NC, 3, 2 * CH, 128), BF16),
            pltpu.VMEM((NC, 4 * CH, KV), BF16),
            pltpu.VMEM((NC, 3, 2 * CH, 128), F32),
            pltpu.VMEM((NC, 3, 2 * CH, 128), F32),
            pltpu.VMEM((ROWS, 2 * KV), BF16),
            pltpu.VMEM((NC, CH, PAD), BF16),
            pltpu.VMEM((NC, CH, PAD), BF16),
            pltpu.VMEM((ROWS, PAD), F32),
            pltpu.VMEM((ROWS, PAD), F32),
            pltpu.VMEM((NC, 8, CH), F32),
            pltpu.VMEM((NC, 3, 8, CH), F32),
            dma, dma, dma,
            dma((NC, 2)), dma((NC, 2)), dma((NC, 2)), dma((NC, 2)),
            dma((3, 4)), dma((2,)), dma((2,)), dma((2,)),
            dma((3, NC)), dma((3, NC)),
            dma((NC,)), dma((NC,)), dma((NC,)), dma((NC,)),
            dma((NC, 3)), dma((NC, 3)),
        ],
        compiler_params=pltpu.CompilerParams(
            collective_id=0, has_side_effects=True, vmem_limit_bytes=60 * 1024 * 1024
        ),
        cost_estimate=pl.CostEstimate(flops=12_000_000_000, bytes_accessed=28_000_000, transcendentals=3_000_000),
    )(
        tokens.T,
        positions.reshape(1, ROWS),
        w_query,
        w_key,
        w_value,
        w_out,
        gain_input.reshape(1, WIDTH),
        gain_query.reshape(1, 128),
        gain_key.reshape(1, 128),
        gain_post.reshape(1, WIDTH),
        gain_pre.reshape(1, WIDTH),
    )


def solution(mesh):
    torus = Mesh(mesh.devices.reshape(N_SEQ, 2, 2), ("seq", "tp_0", "tp_1"))
    tp = ("tp_0", "tp_1")
    return jax.shard_map(
        local,
        mesh=torus,
        in_specs=(
            P("seq", tp), P("seq"), P(None, tp), P(None, tp), P(None, tp), P(tp, None),
            P(), P(), P(), P(), P(),
        ),
        out_specs=(P("seq", tp), P("seq", tp)),
        check_vma=False,
    )
```

time: 205 us -> 130 us (0.63)
  the two profiles are of different devices: /device:TPU:65 before, /device:TPU:5 now
where the time goes in v1:
time: 130 us
  Pallas kernels  119 us (92%)
  local copies, waits for them, and re-layouts  9.99 us (8%)
    pallas_call x1, Pallas kernels, local(): pl.pallas_call(kernel, out_shape=(out, out), in_specs=[hbm, vmem, hbm, hb...  119 us
    pallas_call x2, local copies, waits for them, and re-layouts, local(): pl.pallas_call(kernel, out_shape=(out, out), in_specs=[hbm, vmem, hbm, hb...  4.65 us

profile of v1, /device:TPU:5, one launch (start us, length us, event | category | flops | bytes accessed | tf_op | source)
XLA Modules:
  0.0 129.8 jit_solution(16584490605023217261)
XLA Ops:
  0.6 1.3 reshape.22.pos
  1.9 1.4 %reshape.23.gi = f32[1,5376]{1,0:T(1,128)} reshape(f32[5376]{0:T(1024)} %param.17) | data formatting | bytes 43008 | tf_op jit(solution)/shard_map/reshape | solution.py:391
  3.2 1.4 %reshape.26.gpost = f32[1,5376]{1,0:T(1,128)} reshape(f32[5376]{0:T(1024)} %param.20) | data formatting | bytes 43008 | tf_op jit(solution)/shard_map/reshape | solution.py:394
  4.6 1.4 %reshape.27.gpre = f32[1,5376]{1,0:T(1,128)} reshape(f32[5376]{0:T(1024)} %param.21) | data formatting | bytes 43008 | tf_op jit(solution)/shard_map/reshape | solution.py:395
  6.0 119.2 %shard_map.122 = (bf16[384,1344]{1,0:T(8,128)(2,1)}, bf16[384,1344]{1,0:T(8,128)(2,1)}) custom-call(bf16[1344,384]{1,0:T(8,128)(2,1)} %bitcast.3, s32[1,384]{1,0:T(1,128)} %reshape.22.pos, bf16[5376,768]{1,0:T(8,128)(2,1)} %wq.1, bf16[5376,384]{1,0:T(8,128)(2,1)} %wk.1, bf16[5376,384]{1,0:T(8,128)(2,1)} %wv.1, bf16[768,5376]{1,0:T(8,128)(2,1)} %wo.1, ...), custom_call_target="tpu_custom_call" | custom-call | flops 12000000000 | bytes 28000000 | tf_op jit(solution)/shard_map/pallas_call | solution.py:345
  125.1 2.3 %copy.13 = bf16[384,1344]{0,1:T(8,128)(2,1)} copy(bf16[384,1344]{1,0:T(8,128)(2,1)} %get-tuple-element.2) | data formatting | bytes 2064384 | tf_op jit(solution)/shard_map/pallas_call | solution.py:345
  127.5 2.3 %copy.14 = bf16[384,1344]{0,1:T(8,128)(2,1)} copy(bf16[384,1344]{1,0:T(8,128)(2,1)} %get-tuple-element.3) | data formatting | bytes 2064384 | tf_op jit(solution)/shard_map/pallas_call | solution.py:345

commit v2 on v1

--- a/solution.py
+++ b/solution.py
@@ -30,9 +30,9 @@
     xt, pos, wq, wk, wv, wo, gi, gq, gk, gpost, gpre,
     hid, ffn,
     xg, wqv, wkv, wvv, wov, acc, ss, gtab, rope_c, rope_s, bias,
-    qs, kvb, o_acc, l_acc, att, rs_send, rs_recv, own, tok, st_send, st_recv,
+    qs, kvb, o_acc, l_acc, att, rs_send, rs_recv, own, tok, st_send, st_recv, stage,
     s_own, s_sib, r_sib, s_z, r_z, s_f, r_f, s_w, s_wo, s_wos, r_wos,
-    s_kv, r_kv, s_at, r_at, s_rs, r_rs, s_st, r_st,
+    s_kv, r_kv, s_stage, r_stage, s_pass, r_pass, s_at, r_at, s_rs, r_rs, s_st, r_st,
 ):
     seq = lax.axis_index("seq")
     zl = lax.axis_index("tp_0")
@@ -48,15 +48,16 @@
         t = tp_of(k)
         return pl.multiple_of(OWN * t - 64 * lax.rem(t, 2), 128)
 
-    def later(k):
-        return (lax.rem(seq + k, N_SEQ), zl, core)
+    def later(k, dz=0):
+        return (lax.rem(seq + k, N_SEQ), lax.rem(zl + dz, 2), core)
 
     barrier = pltpu.get_barrier_semaphore()
     for k in (1, 2, 3):
         pl.semaphore_signal(barrier, inc=1, device_id=peer(k), device_id_type=MESH)
-        pl.semaphore_signal(barrier, inc=1, device_id=later(k), device_id_type=MESH)
-        pl.semaphore_signal(barrier, inc=1, device_id=later(N_SEQ - k), device_id_type=MESH)
-    pl.semaphore_wait(barrier, 9)
+    for k in (1, 3, N_SEQ - 1, N_SEQ - 3):
+        for dz in (0, 1):
+            pl.semaphore_signal(barrier, inc=1, device_id=later(k, dz), device_id_type=MESH)
+    pl.semaphore_wait(barrier, 11)
 
     def remote(src, dst, ss_, rs_, dev):
         return pltpu.make_async_remote_copy(
@@ -91,14 +92,146 @@
         for i, k in enumerate((3, 1))
     ]
 
-    def kv_copy(k, c):
+    def kv_copy(back, ahead, c):
+        far = (back + ahead) % N_SEQ
         return remote(
-            kvb.at[c, pl.ds(3 * CH, CH)],
-            kvb.at[c, pl.ds((3 - k) * CH, CH)],
-            s_kv.at[k - 1, c],
-            r_kv.at[k - 1, c],
-            later(k),
+            kvb.at[c, pl.ds((3 - back) * CH, CH)],
+            kvb.at[c, pl.ds((3 - far) * CH, CH)],
+            s_kv.at[3 if back == 3 else far - 1, c],
+            r_kv.at[far - 1, c],
+            later(ahead),
         )
+
+    seq16 = lax.rem(seq, 16)
+    crossing = (seq16 >= 13) & (seq < 16)
+
+    def key_copy(ahead, c):
+        return remote(
+            kvb.at[c, pl.ds(3 * CH, CH), pl.ds(0, 384)],
+            kvb.at[c, pl.ds((3 - ahead) * CH, CH), pl.ds(0, 384)],
+            s_kv.at[ahead - 1, c],
+            r_kv.at[ahead - 1, c],
+            later(ahead),
+        )
+
+    def value_copy(ahead, c):
+        return remote(
+            kvb.at[c, pl.ds(3 * CH, CH), pl.ds(384, 384)],
+            stage.at[ahead // 2, c],
+            s_stage.at[ahead // 2, c],
+            r_stage.at[ahead // 2, c],
+            later(ahead, 1),
+        )
+
+    def value_pass(ahead, c):
+        return remote(
+            stage.at[ahead // 2, c],
+            kvb.at[c, pl.ds((3 - ahead) * CH, CH), pl.ds(384, 384)],
+            s_pass.at[ahead // 2, c],
+            r_pass.at[ahead // 2, c],
+            peer(2),
+        )
+
+    def sends(ahead, c):
+        if ahead == 3 and c == 0:
+            return seq == 14
+        return seq < N_SEQ - ahead
+
+    def crosses(ahead, c):
+        if ahead == 1:
+            return seq == 15
+        return (seq == 14) if c == 0 else crossing
+
+    def crossed(ahead, c):
+        if ahead == 1:
+            return seq == 16
+        return (seq == 17) if c == 0 else (seq >= 16) & (seq < 19)
+
+    def relays_on(c):
+        on = (seq >= 1) & (seq < N_SEQ - 1)
+        return on & (seq != 15) if c == 0 else on & (seq16 == 14)
+
+    def relays_back(c):
+        return (seq == 17) if c == 0 else (seq >= 3) & (seq16 != 0)
+
+    def send_kv(ahead, c):
+        @pl.when(sends(ahead, c) & jnp.logical_not(crosses(ahead, c)))
+        def _():
+            kv_copy(0, ahead, c).start()
+
+    def send_values(ahead, c):
+        @pl.when(crosses(ahead, c))
+        def _():
+            value_copy(ahead, c).start()
+
+    def send_keys(ahead, c):
+        @pl.when(crosses(ahead, c))
+        def _():
+            key_copy(ahead, c).start()
+
+    def pass_values(ahead, c):
+        @pl.when(crossed(ahead, c))
+        def _():
+            value_copy(ahead, c).wait_recv()
+            value_pass(ahead, c).start()
+
+    def got_kv(ahead, c, other):
+        @pl.when(other & crossed(ahead, c))
+        def _():
+            key_copy(ahead, c).wait_recv()
+            value_pass(ahead, c).wait_recv()
+
+        first = (seq >= 1) if ahead == 1 else (seq >= 3) if c > 0 else (seq < 0)
+
+        @pl.when(other & first & jnp.logical_not(crossed(ahead, c)))
+        def _():
+            kv_copy(0, ahead, c).wait_recv()
+
+    def relay_on(c, some=True):
+        got_kv(1, c, relays_on(c) & some)
+
+        @pl.when(relays_on(c) & some)
+        def _():
+            kv_copy(1, 1, c).start()
+
+    def relay_back(c):
+        got_kv(3, c, relays_back(c))
+
+        @pl.when(relays_back(c))
+        def _():
+            kv_copy(3, N_SEQ - 1, c).start()
+
+    def kv_arrived(c):
+        got_kv(1, c, jnp.logical_not(relays_on(c)))
+
+        @pl.when(seq >= 2)
+        def _():
+            kv_copy(1, 1, c).wait_recv()
+
+        got_kv(3, c, jnp.logical_not(relays_back(c)))
+
+    def kv_left(c):
+        for ahead in (1, 3):
+            @pl.when(sends(ahead, c) & jnp.logical_not(crosses(ahead, c)))
+            def _():
+                kv_copy(0, ahead, c).wait_send()
+
+            @pl.when(crosses(ahead, c))
+            def _():
+                value_copy(ahead, c).wait_send()
+                key_copy(ahead, c).wait_send()
+
+            @pl.when(crossed(ahead, c))
+            def _():
+                value_pass(ahead, c).wait_send()
+
+        @pl.when(relays_on(c))
+        def _():
+            kv_copy(1, 1, c).wait_send()
+
+        @pl.when(relays_back(c))
+        def _():
+            kv_copy(3, N_SEQ - 1, c).wait_send()
 
     def att_copy(c):
         return remote(
@@ -133,19 +266,19 @@
     for k in (1, 2, 3):
         @pl.when(seq < k)
         def _():
-            for c in range(NC):
+            for c in range(1 if k == 3 else 0, NC):
                 kvb[c, pl.ds((3 - k) * CH, CH), :] = jnp.zeros((CH, KV), BF16)
-    kvb[0, pl.ds(0, CH), :] = jnp.zeros((CH, KV), BF16)
-
+
+    gi_row = gi[...].reshape(1, WIDTH)
     for i in range(8):
-        gtab[i] = jnp.broadcast_to(gi[:, pl.ds(i * HALF, HALF)], (8, HALF))
+        gtab[i] = jnp.broadcast_to(gi_row[:, i * HALF : (i + 1) * HALF], (8, HALF))
 
     lane = lax.broadcasted_iota(jnp.int32, (CH, CH), 1)
     sub = lax.broadcasted_iota(jnp.int32, (CH, CH), 0)
     half_lane = jnp.where(lane >= 64, lane - 64, lane).astype(F32)
     inverse_freq = jnp.exp(half_lane * (-math.log(10000.0) / 64))
     for c in range(NC):
-        p_row = pos[:, pl.ds(c * CH, CH)].astype(F32)
+        p_row = pos[pl.ds(c * CH, CH)].reshape(1, CH).astype(F32)
         p_mat = jnp.broadcast_to(p_row, (CH, CH)).T
         angle = p_mat * inverse_freq
         sine = jnp.sin(angle)
@@ -202,20 +335,18 @@
         scale = jnp.broadcast_to(lax.rsqrt(mean + EPS), (CH, CH)).T
         for h in range(3):
             u = acc[rows, pl.ds(768 + h * 128, 128)] * scale
-            kvb[c, pl.ds(3 * CH, CH), pl.ds(h * 128, 128)] = head(u, gk[...], c)
+            kvb[c, pl.ds(3 * CH, CH), pl.ds(h * 128, 128)] = head(u, gk[...].reshape(1, 128), c)
             v = acc[rows, pl.ds(1152 + h * 128, 128)] * scale
             kvb[c, pl.ds(3 * CH, CH), pl.ds(384 + h * 128, 128)] = v.astype(BF16)
-        for k in (1, 2, 3):
-            if k == 3 and c == 0:
-                continue
-
-            @pl.when(seq + k < N_SEQ)
-            def _():
-                kv_copy(k, c).start()
+
+    def finish_q(c):
+        rows = pl.ds(c * CH, CH)
+        mean = ss[c, pl.ds(0, 1), :] / WIDTH
+        scale = jnp.broadcast_to(lax.rsqrt(mean + EPS), (CH, CH)).T
         for h in range(3):
             for g in range(2):
                 u = acc[rows, pl.ds((2 * h + g) * 128, 128)] * scale
-                qs[c, h, pl.ds(g * CH, CH), :] = head(u, gq[...], c)
+                qs[c, h, pl.ds(g * CH, CH), :] = head(u, gq[...].reshape(1, 128), c)
 
     for c in range(NC):
         @pl.loop(0, 2)
@@ -227,6 +358,22 @@
             step(3, c, h)
 
         finish(c)
+        for ahead in (1, 3):
+            send_kv(ahead, c)
+            send_values(ahead, c)
+            if c != 1:
+                send_keys(ahead, c)
+        if c == 1:
+            relay_on(0, seq != 16)
+        if c == 2:
+            for ahead in (1, 3):
+                send_keys(ahead, 1)
+            for early in (0, 1):
+                for ahead in (1, 3):
+                    pass_values(ahead, early)
+            relay_on(0, seq == 16)
+            relay_back(0)
+        finish_q(c)
 
     def unit(c, cc):
         start = 0 if cc > c else CH
@@ -240,19 +387,18 @@
             l_acc[c, h] += w[:, 0:128] + w[:, 128:256] + w[:, 256:384]
             o_acc[c, h] += jnp.dot(w.astype(BF16), vals, preferred_element_type=F32)
 
-    def kv_arrived(cc):
-        for k in (1, 2, 3):
-            if k == 3 and cc == 0:
-                continue
-
-            @pl.when(seq >= k)
-            def _():
-                kv_copy(k, cc).wait_recv()
-
-    for cc in range(2):
-        kv_arrived(cc)
-        for c in range(NC):
-            unit(c, cc)
+    relay_on(1)
+    relay_back(1)
+    kv_arrived(0)
+    for c in range(NC):
+        unit(c, 0)
+    for ahead in (1, 3):
+        pass_values(ahead, 2)
+    relay_on(2)
+    relay_back(2)
+    kv_arrived(1)
+    for c in range(NC):
+        unit(c, 1)
     kv_arrived(2)
     for cp in wo_copies:
         cp.wait()
@@ -281,8 +427,8 @@
     for c in range(NC):
         own[pl.ds(c * CH, CH), :] = project(c, 1)
 
-    gain_post = gpost[:, pl.ds(col_start(0), PAD)]
-    gain_pre = gpre[:, pl.ds(col_start(0), PAD)]
+    gain_post = gpost[pl.ds(col_start(0), PAD)].reshape(1, PAD)
+    gain_pre = gpre[pl.ds(col_start(0), PAD)].reshape(1, PAD)
     col = lax.broadcasted_iota(jnp.int32, (1, PAD), 1) - 64 * core
     inside = ((col >= 0) & (col < OWN)).astype(F32)
 
@@ -313,10 +459,10 @@
         out = hidden * pre * gain_pre
 
         def place(v):
-            return jnp.where(core == 1, pltpu.roll(v, PAD - 64, 1), v)[:, :OWN].astype(BF16)
-
-        hid[rows, :] = place(hidden)
-        ffn[rows, :] = place(out)
+            return jnp.where(core == 1, pltpu.roll(v, PAD - 64, 1), v)[:, :OWN].T.astype(BF16)
+
+        hid[:, rows] = place(hidden)
+        ffn[:, rows] = place(out)
 
     for c in range(NC):
         stats(c)
@@ -328,11 +474,9 @@
             z_copy(c, h).wait_send()
             f_copy(c, h).wait_send()
         for k in (1, 2, 3):
-            if not (k == 3 and c == 0):
-                @pl.when(seq + k < N_SEQ)
-                def _():
-                    kv_copy(k, c).wait_send()
             st_copy(c, k).wait_send()
+
+        kv_left(c)
         att_copy(c).wait_send()
         rs_copy(c).wait_send()
 
@@ -341,8 +485,8 @@
     hbm = pl.BlockSpec(memory_space=pltpu.MemorySpace.HBM)
     vmem = pl.BlockSpec(memory_space=pltpu.VMEM)
     dma = pltpu.SemaphoreType.DMA
-    out = jax.ShapeDtypeStruct((ROWS, OWN), BF16)
-    return pl.pallas_call(
+    out = jax.ShapeDtypeStruct((OWN, ROWS), BF16)
+    hidden, ffn_input = pl.pallas_call(
         kernel,
         out_shape=(out, out),
         in_specs=[hbm, vmem, hbm, hbm, hbm, hbm, vmem, vmem, vmem, vmem, vmem],
@@ -370,10 +514,12 @@
             pltpu.VMEM((ROWS, PAD), F32),
             pltpu.VMEM((NC, 8, CH), F32),
             pltpu.VMEM((NC, 3, 8, CH), F32),
+            pltpu.VMEM((2, NC, CH, 384), BF16),
             dma, dma, dma,
             dma((NC, 2)), dma((NC, 2)), dma((NC, 2)), dma((NC, 2)),
             dma((3, 4)), dma((2,)), dma((2,)), dma((2,)),
-            dma((3, NC)), dma((3, NC)),
+            dma((4, NC)), dma((3, NC)),
+            dma((2, NC)), dma((2, NC)), dma((2, NC)), dma((2, NC)),
             dma((NC,)), dma((NC,)), dma((NC,)), dma((NC,)),
             dma((NC, 3)), dma((NC, 3)),
         ],
@@ -383,17 +529,18 @@
         cost_estimate=pl.CostEstimate(flops=12_000_000_000, bytes_accessed=28_000_000, transcendentals=3_000_000),
     )(
         tokens.T,
-        positions.reshape(1, ROWS),
+        positions,
         w_query,
         w_key,
         w_value,
         w_out,
-        gain_input.reshape(1, WIDTH),
-        gain_query.reshape(1, 128),
-        gain_key.reshape(1, 128),
-        gain_post.reshape(1, WIDTH),
-        gain_pre.reshape(1, WIDTH),
+        gain_input,
+        gain_query,
+        gain_key,
+        gain_post,
+        gain_pre,
     )
+    return hidden.T, ffn_input.T
 
 
 def solution(mesh):

time: 130 us -> 104 us (0.80)
  the two profiles are of different devices: /device:TPU:5 before, /device:TPU:65 now
where the time goes in v2:
time: 104 us; the launch traced here: 103 us
  Pallas kernels  98.2 us (94%)
  local copies, waits for them, and re-layouts  4.56 us (4%)
    pallas_call x1, Pallas kernels, local(): pl.pallas_call(kernel, out_shape=(out, out), in_specs=[hbm, vmem, hbm, hb...  98.2 us
    unnamed x2, local copies, waits for them, and re-layouts  4.56 us

profile of v2, /device:TPU:65, one launch (start us, length us, event | category | flops | bytes accessed | tf_op | source)
XLA Modules:
  0.0 103.4 jit_solution(2564166380506610043)
XLA Ops:
  0.6 98.2 %shard_map.122 = (bf16[1344,384]{1,0:T(8,128)(2,1)}, bf16[1344,384]{1,0:T(8,128)(2,1)}) custom-call(bf16[1344,384]{1,0:T(8,128)(2,1)} %bitcast.5, s32[384]{0:T(512)} %pos.1, bf16[5376,768]{1,0:T(8,128)(2,1)} %wq.1, bf16[5376,384]{1,0:T(8,128)(2,1)} %wk.1, bf16[5376,384]{1,0:T(8,128)(2,1)} %wv.1, bf16[768,5376]{1,0:T(8,128)(2,1)} %wo.1, f32[5376]{0:T(1024)} %gi.1, ...), custom_call_target="tpu_custom_call" | custom-call | flops 12000000000 | bytes 28000000 | tf_op jit(solution)/shard_map/pallas_call | solution.py:489
  98.8 2.3 %copy.15 = bf16[384,1344]{0,1:T(8,128)(2,1)} copy(bf16[384,1344]{0,1:T(8,128)(2,1)} %bitcast.4) | data formatting | bytes 2064384
  101.1 2.3 %copy.16 = bf16[384,1344]{0,1:T(8,128)(2,1)} copy(bf16[384,1344]{0,1:T(8,128)(2,1)} %bitcast.3) | data formatting | bytes 2064384

commit v3 on v2

--- a/solution.py
+++ b/solution.py
@@ -15,6 +15,7 @@
 
 EPS = 1e-6
 WIDTH = 5376
+PARTS = 4
 OWN = 1344
 HALF = 672
 PAD = 1408
@@ -30,9 +31,9 @@
     xt, pos, wq, wk, wv, wo, gi, gq, gk, gpost, gpre,
     hid, ffn,
     xg, wqv, wkv, wvv, wov, acc, ss, gtab, rope_c, rope_s, bias,
-    qs, kvb, o_acc, l_acc, att, rs_send, rs_recv, own, tok, st_send, st_recv, stage,
+    qs, kvb, o_acc, l_acc, att, rs_send, rs_recv, own, post_t, pre_t, turned, hid_v, ffn_v, st_send, st_recv, stage,
     s_own, s_sib, r_sib, s_z, r_z, s_f, r_f, s_w, s_wo, s_wos, r_wos,
-    s_kv, r_kv, s_stage, r_stage, s_pass, r_pass, s_at, r_at, s_rs, r_rs, s_st, r_st,
+    s_kv, r_kv, s_stage, r_stage, s_pass, r_pass, s_at, r_at, s_rs, r_rs, s_st, r_st, s_out,
 ):
     seq = lax.axis_index("seq")
     zl = lax.axis_index("tp_0")
@@ -52,12 +53,27 @@
         return (lax.rem(seq + k, N_SEQ), lax.rem(zl + dz, 2), core)
 
     barrier = pltpu.get_barrier_semaphore()
+    halves = jnp.where((seq >= 13) & (seq < 19), 1, 0) + jnp.where((seq == 15) | (seq == 16), 1, 0)
+    partners = 3 + halves
     for k in (1, 2, 3):
         pl.semaphore_signal(barrier, inc=1, device_id=peer(k), device_id_type=MESH)
-    for k in (1, 3, N_SEQ - 1, N_SEQ - 3):
-        for dz in (0, 1):
-            pl.semaphore_signal(barrier, inc=1, device_id=later(k, dz), device_id_type=MESH)
-    pl.semaphore_wait(barrier, 11)
+    for k in (1, 3):
+        for there, step_to in ((seq + k < N_SEQ, k), (seq >= k, N_SEQ - k)):
+            partners += jnp.where(there, 1, 0)
+
+            @pl.when(there)
+            def _():
+                pl.semaphore_signal(barrier, inc=1, device_id=later(step_to), device_id_type=MESH)
+
+    for there, step_to in (
+        ((seq >= 13) & (seq < 16), 3),
+        ((seq >= 16) & (seq < 19), N_SEQ - 3),
+        (seq == 15, 1),
+        (seq == 16, N_SEQ - 1),
+    ):
+        @pl.when(there)
+        def _():
+            pl.semaphore_signal(barrier, inc=1, device_id=later(step_to, 1), device_id_type=MESH)
 
     def remote(src, dst, ss_, rs_, dev):
         return pltpu.make_async_remote_copy(
@@ -248,12 +264,16 @@
     def st_copy(c, k):
         return remote(st_send.at[c], st_recv.at[c, k - 1], s_st.at[c, k - 1], r_st.at[c, k - 1], peer(k))
 
+    own_copy.start()
+    for k in range(2):
+        for cp in w_copies(k):
+            cp.start()
+    pl.semaphore_wait(barrier, partners)
     for c in range(NC):
         for h in range(2):
             z_copy(c, h).start()
-    own_copy.start()
     sib_copy.start()
-    for k in range(4):
+    for k in (2, 3):
         for cp in w_copies(k):
             cp.start()
     for cp in wo_copies + wo_remote:
@@ -292,11 +312,15 @@
                 j_rel = CH * cc + ROWS * (n - first) + lane
                 bias[c, cc, :, pl.ds(n * CH, CH)] = jnp.where((j_rel >= low) & (j_rel <= i_rel), 0.0, -1e30)
 
+    def own_rows(wide):
+        turned[...] = wide.T
+        return turned.at[pl.ds(pl.multiple_of(64 * core, 64), OWN)]
+
+    for gain, table in ((gpost, post_t), (gpre, pre_t)):
+        row = gain[pl.ds(col_start(0), PAD)].reshape(1, PAD)
+        table[...] = own_rows(jnp.broadcast_to(row, (CH, PAD)))[...]
+
     own_copy.wait()
-    for c in range(NC):
-        x = xg[0, :, pl.ds(c * CH, CH)].astype(F32).T
-        x = jnp.concatenate([x, jnp.zeros((CH, PAD - OWN), F32)], axis=1)
-        tok[pl.ds(c * CH, CH), :] = jnp.where(core == 1, pltpu.roll(x, 64, 1), x)
 
     def step(k, c, h):
         cols = pl.ds(pl.multiple_of(c * CH, CH), CH)
@@ -418,55 +442,72 @@
         att_copy(c).start()
         if c > 0:
             att_copy(c - 1).wait_recv()
-            rs_send[c - 1] = project(c - 1, 0).astype(BF16)
+            rs_send[c - 1] = own_rows(project(c - 1, 0))[...].astype(BF16)
             rs_copy(c - 1).start()
     att_copy(2).wait_recv()
-    rs_send[2] = project(2, 0).astype(BF16)
+    rs_send[2] = own_rows(project(2, 0))[...].astype(BF16)
     rs_copy(2).start()
 
     for c in range(NC):
-        own[pl.ds(c * CH, CH), :] = project(c, 1)
-
-    gain_post = gpost[pl.ds(col_start(0), PAD)].reshape(1, PAD)
-    gain_pre = gpre[pl.ds(col_start(0), PAD)].reshape(1, PAD)
-    col = lax.broadcasted_iota(jnp.int32, (1, PAD), 1) - 64 * core
-    inside = ((col >= 0) & (col < OWN)).astype(F32)
+        own[c] = own_rows(project(c, 1))[...]
+
+    BLOCK = 64
 
     def stats(c):
-        rows = pl.ds(c * CH, CH)
+        cols = pl.ds(c * CH, CH)
         rs_copy(c).wait_recv()
-        s = (own[rows, :] + rs_recv[c].astype(F32)) * inside
-        own[rows, :] = s
-        t = tok[rows, :]
-        sg = s * gain_post
-        both = [jnp.sum(v, axis=-1, keepdims=True) for v in (s * s, t * t, t * sg, sg * sg)]
-        table = jnp.where(lane == 0, both[0], jnp.where(lane == 1, both[1], jnp.where(lane == 2, both[2], both[3])))
-        st_send[c] = table.T[0:8, :]
+
+        def one(i, sums):
+            rows = pl.ds(pl.multiple_of(i * BLOCK, BLOCK), BLOCK)
+            s = own[c, rows, :] + rs_recv[c, rows, :].astype(F32)
+            t = xg[0, rows, cols].astype(F32)
+            sg = s * post_t[rows, :]
+            own[c, rows, :] = s
+            return tuple(
+                a + jnp.sum((u * v).reshape(BLOCK // 8, 8, CH), axis=0)
+                for a, u, v in zip(sums, (s, t, t, sg), (s, t, sg, sg))
+            )
+
+        sums = lax.fori_loop(0, OWN // BLOCK, one, (jnp.zeros((8, CH), F32),) * 4)
+        for i, v in enumerate(sums):
+            st_send[c, pl.ds(i, 1), :] = jnp.sum(v, axis=0, keepdims=True)
+        for i in range(4, 8):
+            st_send[c, pl.ds(i, 1), :] = jnp.zeros((1, CH), F32)
         for k in (1, 2, 3):
             st_copy(c, k).start()
 
     def final(c):
-        rows = pl.ds(c * CH, CH)
+        cols = pl.ds(c * CH, CH)
         for k in (1, 2, 3):
             st_copy(c, k).wait_recv()
         rows4 = st_send[c] + st_recv[c, 0] + st_recv[c, 1] + st_recv[c, 2]
         post = lax.rsqrt(rows4[0:1] / WIDTH + EPS)
         square = rows4[1:2] + 2.0 * post * rows4[2:3] + post * post * rows4[3:4]
         pre = lax.rsqrt(jnp.maximum(square, 0.0) / WIDTH + EPS)
-        post = jnp.broadcast_to(post, (CH, CH)).T[:, 0:1]
-        pre = jnp.broadcast_to(pre, (CH, CH)).T[:, 0:1]
-        hidden = (tok[rows, :] + own[rows, :] * post * gain_post).astype(BF16).astype(F32)
-        out = hidden * pre * gain_pre
-
-        def place(v):
-            return jnp.where(core == 1, pltpu.roll(v, PAD - 64, 1), v)[:, :OWN].T.astype(BF16)
-
-        hid[:, rows] = place(hidden)
-        ffn[:, rows] = place(out)
+
+        @pl.loop(0, OWN // BLOCK)
+        def _(i):
+            rows = pl.ds(pl.multiple_of(i * BLOCK, BLOCK), BLOCK)
+            t = xg[0, rows, cols].astype(F32)
+            hidden = (t + own[c, rows, :] * post * post_t[rows, :]).astype(BF16)
+            hid_v[rows, cols] = hidden
+            ffn_v[rows, cols] = (hidden.astype(F32) * pre * pre_t[rows, :]).astype(BF16)
+
+        for cp in out_copies(c):
+            cp.start()
+
+    def out_copies(c):
+        cols = pl.ds(c * CH, CH)
+        return [
+            pltpu.make_async_copy(hid_v.at[:, cols], hid.at[:, cols], s_out.at[0, c]),
+            pltpu.make_async_copy(ffn_v.at[:, cols], ffn.at[:, cols], s_out.at[1, c]),
+        ]
 
     for c in range(NC):
         stats(c)
-        final(c)
+        if c > 0:
+            final(c - 1)
+    final(NC - 1)
 
     sib_copy.wait_send()
     for c in range(NC):
@@ -479,6 +520,27 @@
         kv_left(c)
         att_copy(c).wait_send()
         rs_copy(c).wait_send()
+        for cp in out_copies(c):
+            cp.wait()
+
+
+def copy_out(hidden, ffn_input, hid, ffn, buf, sem_in, sem_out):
+    part = OWN // PARTS
+    pieces = [
+        (
+            pltpu.make_async_copy(a.at[pl.ds(i * part, part)], buf.at[n, pl.ds(i * part, part)], sem_in.at[n, i]),
+            pltpu.make_async_copy(buf.at[n, pl.ds(i * part, part)], b.at[pl.ds(i * part, part)], sem_out.at[n, i]),
+        )
+        for n, (a, b) in enumerate(((hidden, hid), (ffn_input, ffn)))
+        for i in range(PARTS)
+    ]
+    for into, _ in pieces:
+        into.start()
+    for into, away in pieces:
+        into.wait()
+        away.start()
+    for _, away in pieces:
+        away.wait()
 
 
 def local(tokens, positions, w_query, w_key, w_value, w_out, gain_input, gain_query, gain_key, gain_post, gain_pre):
@@ -490,7 +552,7 @@
         kernel,
         out_shape=(out, out),
         in_specs=[hbm, vmem, hbm, hbm, hbm, hbm, vmem, vmem, vmem, vmem, vmem],
-        out_specs=(vmem, vmem),
+        out_specs=(hbm, hbm),
         scratch_shapes=[
             pltpu.VMEM((4, OWN, ROWS), BF16),
             pltpu.VMEM((4, OWN, 768), BF16),
@@ -508,10 +570,14 @@
             pltpu.VMEM((NC, 3, 2 * CH, 128), F32),
             pltpu.VMEM((NC, 3, 2 * CH, 128), F32),
             pltpu.VMEM((ROWS, 2 * KV), BF16),
-            pltpu.VMEM((NC, CH, PAD), BF16),
-            pltpu.VMEM((NC, CH, PAD), BF16),
-            pltpu.VMEM((ROWS, PAD), F32),
-            pltpu.VMEM((ROWS, PAD), F32),
+            pltpu.VMEM((NC, OWN, CH), BF16),
+            pltpu.VMEM((NC, OWN, CH), BF16),
+            pltpu.VMEM((NC, OWN, CH), F32),
+            pltpu.VMEM((OWN, CH), F32),
+            pltpu.VMEM((OWN, CH), F32),
+            pltpu.VMEM((PAD, CH), F32),
+            pltpu.VMEM((OWN, ROWS), BF16),
+            pltpu.VMEM((OWN, ROWS), BF16),
             pltpu.VMEM((NC, 8, CH), F32),
             pltpu.VMEM((NC, 3, 8, CH), F32),
             pltpu.VMEM((2, NC, CH, 384), BF16),
@@ -521,7 +587,7 @@
             dma((4, NC)), dma((3, NC)),
             dma((2, NC)), dma((2, NC)), dma((2, NC)), dma((2, NC)),
             dma((NC,)), dma((NC,)), dma((NC,)), dma((NC,)),
-            dma((NC, 3)), dma((NC, 3)),
+            dma((NC, 3)), dma((NC, 3)), dma((2, NC)),
         ],
         compiler_params=pltpu.CompilerParams(
             collective_id=0, has_side_effects=True, vmem_limit_bytes=60 * 1024 * 1024
@@ -540,7 +606,15 @@
         gain_post,
         gain_pre,
     )
-    return hidden.T, ffn_input.T
+    copied = pl.pallas_call(
+        copy_out,
+        out_shape=(out, out),
+        in_specs=[hbm, hbm],
+        out_specs=(hbm, hbm),
+        scratch_shapes=[pltpu.VMEM((2, OWN, ROWS), BF16), dma((2, PARTS)), dma((2, PARTS))],
+        compiler_params=pltpu.CompilerParams(has_side_effects=True),
+    )(hidden, ffn_input)
+    return copied[0].T, copied[1].T
 
 
 def solution(mesh):

time: 104 us -> 95.9 us (0.922)
  local copies, waits for them, and re-layouts: 4.56 us -> 0 us
  Pallas kernels: 98.2 us -> 94.9 us
    pallas_call x1, Pallas kernels: 98.2 us -> 92.4 us  [local(): pl.pallas_call(kernel, out_shape=(out, out), in_specs=[hbm, vmem, hbm, hb...]
    unnamed x2 -> x0, local copies, waits for them, and re-layouts: 4.56 us -> none
    pallas_call x0 -> x1, Pallas kernels: none -> 2.51 us  [local(): pl.pallas_call(copy_out, out_shape=(out, out), in_specs=[hbm, hbm], out_s...]
where the time goes in v3:
time: 95.9 us; the launch traced here: 95.7 us
  Pallas kernels  94.9 us (99%)
    pallas_call x1, Pallas kernels, local(): pl.pallas_call(kernel, out_shape=(out, out), in_specs=[hbm, vmem, hbm, hb...  92.4 us
    pallas_call x1, Pallas kernels, local(): pl.pallas_call(copy_out, out_shape=(out, out), in_specs=[hbm, hbm], out_s...  2.51 us

profile of v3, /device:TPU:65, one launch (start us, length us, event | category | flops | bytes accessed | tf_op | source)
XLA Modules:
  0.0 95.7 jit_solution(1224484840773206735)
XLA Ops:
  0.6 92.4 %shard_map.122 = (bf16[1344,384]{1,0:T(8,128)(2,1)}, bf16[1344,384]{1,0:T(8,128)(2,1)}) custom-call(bf16[1344,384]{1,0:T(8,128)(2,1)} %bitcast.3, s32[384]{0:T(512)} %pos.1, bf16[5376,768]{1,0:T(8,128)(2,1)} %wq.1, bf16[5376,384]{1,0:T(8,128)(2,1)} %wk.1, bf16[5376,384]{1,0:T(8,128)(2,1)} %wv.1, bf16[768,5376]{1,0:T(8,128)(2,1)} %wo.1, f32[5376]{0:T(1024)} %gi.1, ...), custom_call_target="tpu_custom_call" | custom-call | flops 12000000000 | bytes 28000000 | tf_op jit(solution)/shard_map/pallas_call | solution.py:551
  93.1 2.5 %shard_map.123 = (bf16[1344,384]{1,0:T(8,128)(2,1)}, bf16[1344,384]{1,0:T(8,128)(2,1)}) custom-call(bf16[1344,384]{1,0:T(8,128)(2,1)} %get-tuple-element.6.hidden, bf16[1344,384]{1,0:T(8,128)(2,1)} %get-tuple-element.7.ffn_input), custom_call_target="tpu_custom_call" | custom-call | tf_op jit(solution)/shard_map/pallas_call | solution.py:609

commit v4 on v3

--- a/solution.py
+++ b/solution.py
@@ -33,7 +33,7 @@
     xg, wqv, wkv, wvv, wov, acc, ss, gtab, rope_c, rope_s, bias,
     qs, kvb, o_acc, l_acc, att, rs_send, rs_recv, own, post_t, pre_t, turned, hid_v, ffn_v, st_send, st_recv, stage,
     s_own, s_sib, r_sib, s_z, r_z, s_f, r_f, s_w, s_wo, s_wos, r_wos,
-    s_kv, r_kv, s_stage, r_stage, s_pass, r_pass, s_at, r_at, s_rs, r_rs, s_st, r_st, s_out,
+    s_kv, r_kv, s_stage, r_stage, s_pass, s_at, r_at, s_rs, r_rs, s_st, r_st, s_out,
 ):
     seq = lax.axis_index("seq")
     zl = lax.axis_index("tp_0")
@@ -108,27 +108,21 @@
         for i, k in enumerate((3, 1))
     ]
 
-    def kv_copy(back, ahead, c):
+    def kv_copy(back, ahead, c, part):
         far = (back + ahead) % N_SEQ
+        cols = pl.ds(384 * part, 384)
         return remote(
-            kvb.at[c, pl.ds((3 - back) * CH, CH)],
-            kvb.at[c, pl.ds((3 - far) * CH, CH)],
-            s_kv.at[3 if back == 3 else far - 1, c],
-            r_kv.at[far - 1, c],
+            kvb.at[c, pl.ds((3 - back) * CH, CH), cols],
+            kvb.at[c, pl.ds((3 - far) * CH, CH), cols],
+            s_kv.at[3 if back == 3 else far - 1, c, part],
+            r_kv.at[far - 1, c, part],
             later(ahead),
         )
 
+    seq4 = lax.rem(seq, 4)
     seq16 = lax.rem(seq, 16)
-    crossing = (seq16 >= 13) & (seq < 16)
-
-    def key_copy(ahead, c):
-        return remote(
-            kvb.at[c, pl.ds(3 * CH, CH), pl.ds(0, 384)],
-            kvb.at[c, pl.ds((3 - ahead) * CH, CH), pl.ds(0, 384)],
-            s_kv.at[ahead - 1, c],
-            r_kv.at[ahead - 1, c],
-            later(ahead),
-        )
+    before_half = (seq >= 13) & (seq < 16)
+    after_half = (seq >= 16) & (seq < 19)
 
     def value_copy(ahead, c):
         return remote(
@@ -144,110 +138,82 @@
             stage.at[ahead // 2, c],
             kvb.at[c, pl.ds((3 - ahead) * CH, CH), pl.ds(384, 384)],
             s_pass.at[ahead // 2, c],
-            r_pass.at[ahead // 2, c],
+            r_kv.at[ahead - 1, c, 1],
             peer(2),
         )
 
     def sends(ahead, c):
-        if ahead == 3 and c == 0:
-            return seq == 14
-        return seq < N_SEQ - ahead
+        return (seq < N_SEQ - ahead) & (seq4 == 2) if ahead == 3 and c == 0 else seq < N_SEQ - ahead
+
+    def gets(ahead, c):
+        return (seq >= 3) & (seq4 == 1) if ahead == 3 and c == 0 else seq >= ahead
 
     def crosses(ahead, c):
-        if ahead == 1:
-            return seq == 15
-        return (seq == 14) if c == 0 else crossing
+        return seq == 15 if ahead == 1 else before_half & sends(3, c)
 
     def crossed(ahead, c):
-        if ahead == 1:
-            return seq == 16
-        return (seq == 17) if c == 0 else (seq >= 16) & (seq < 19)
+        return seq == 16 if ahead == 1 else after_half & gets(3, c)
 
     def relays_on(c):
         on = (seq >= 1) & (seq < N_SEQ - 1)
-        return on & (seq != 15) if c == 0 else on & (seq16 == 14)
+        return on & (seq4 != 3) if c == 0 else on & (seq16 == 14)
 
     def relays_back(c):
-        return (seq == 17) if c == 0 else (seq >= 3) & (seq16 != 0)
-
-    def send_kv(ahead, c):
-        @pl.when(sends(ahead, c) & jnp.logical_not(crosses(ahead, c)))
+        return (seq >= 3) & (seq4 == 1) if c == 0 else (seq >= 3) & (seq16 != 0)
+
+    def when(condition, action):
+        @pl.when(condition)
         def _():
-            kv_copy(0, ahead, c).start()
-
-    def send_values(ahead, c):
-        @pl.when(crosses(ahead, c))
-        def _():
-            value_copy(ahead, c).start()
-
-    def send_keys(ahead, c):
-        @pl.when(crosses(ahead, c))
-        def _():
-            key_copy(ahead, c).start()
+            action()
+
+    def send_kv(c, part):
+        for ahead in (3, 1):
+            across = crosses(ahead, c)
+            if part == 0 and c == 1:
+                when(sends(ahead, c) & jnp.logical_not(across), kv_copy(0, ahead, c, 0).start)
+            elif part == 0:
+                when(sends(ahead, c), kv_copy(0, ahead, c, 0).start)
+            else:
+                when(sends(ahead, c) & jnp.logical_not(across), kv_copy(0, ahead, c, 1).start)
+                when(across, value_copy(ahead, c).start)
 
     def pass_values(ahead, c):
-        @pl.when(crossed(ahead, c))
-        def _():
+        def act():
             value_copy(ahead, c).wait_recv()
             value_pass(ahead, c).start()
 
-    def got_kv(ahead, c, other):
-        @pl.when(other & crossed(ahead, c))
-        def _():
-            key_copy(ahead, c).wait_recv()
-            value_pass(ahead, c).wait_recv()
-
-        first = (seq >= 1) if ahead == 1 else (seq >= 3) if c > 0 else (seq < 0)
-
-        @pl.when(other & first & jnp.logical_not(crossed(ahead, c)))
-        def _():
-            kv_copy(0, ahead, c).wait_recv()
+        when(crossed(ahead, c), act)
+
+    def relay(relays, back, ahead, c, some):
+        def act():
+            for part in (0, 1):
+                kv_copy(0, back, c, part).wait_recv()
+                kv_copy(back, ahead, c, part).start()
+
+        when(relays(c) & some, act)
 
     def relay_on(c, some=True):
-        got_kv(1, c, relays_on(c) & some)
-
-        @pl.when(relays_on(c) & some)
-        def _():
-            kv_copy(1, 1, c).start()
-
-    def relay_back(c):
-        got_kv(3, c, relays_back(c))
-
-        @pl.when(relays_back(c))
-        def _():
-            kv_copy(3, N_SEQ - 1, c).start()
+        relay(relays_on, 1, 1, c, some)
+
+    def relay_back(c, some=True):
+        relay(relays_back, 3, N_SEQ - 1, c, some)
 
     def kv_arrived(c):
-        got_kv(1, c, jnp.logical_not(relays_on(c)))
-
-        @pl.when(seq >= 2)
-        def _():
-            kv_copy(1, 1, c).wait_recv()
-
-        got_kv(3, c, jnp.logical_not(relays_back(c)))
+        for part in (0, 1):
+            when((seq >= 1) & jnp.logical_not(relays_on(c)), kv_copy(0, 1, c, part).wait_recv)
+            when(seq >= 2, kv_copy(1, 1, c, part).wait_recv)
+            when(gets(3, c) & jnp.logical_not(relays_back(c)), kv_copy(0, 3, c, part).wait_recv)
 
     def kv_left(c):
         for ahead in (1, 3):
-            @pl.when(sends(ahead, c) & jnp.logical_not(crosses(ahead, c)))
-            def _():
-                kv_copy(0, ahead, c).wait_send()
-
-            @pl.when(crosses(ahead, c))
-            def _():
-                value_copy(ahead, c).wait_send()
-                key_copy(ahead, c).wait_send()
-
-            @pl.when(crossed(ahead, c))
-            def _():
-                value_pass(ahead, c).wait_send()
-
-        @pl.when(relays_on(c))
-        def _():
-            kv_copy(1, 1, c).wait_send()
-
-        @pl.when(relays_back(c))
-        def _():
-            kv_copy(3, N_SEQ - 1, c).wait_send()
+            across = crosses(ahead, c)
+            when(sends(ahead, c), kv_copy(0, ahead, c, 0).wait_send)
+            when(sends(ahead, c) & jnp.logical_not(across), kv_copy(0, ahead, c, 1).wait_send)
+            when(across, value_copy(ahead, c).wait_send)
+            when(crossed(ahead, c), value_pass(ahead, c).wait_send)
+        for part in (0, 1):
+            when(relays_on(c), kv_copy(1, 1, c, part).wait_send)
+            when(relays_back(c), kv_copy(3, N_SEQ - 1, c, part).wait_send)
 
     def att_copy(c):
         return remote(
@@ -360,8 +326,11 @@
         for h in range(3):
             u = acc[rows, pl.ds(768 + h * 128, 128)] * scale
             kvb[c, pl.ds(3 * CH, CH), pl.ds(h * 128, 128)] = head(u, gk[...].reshape(1, 128), c)
+        send_kv(c, 0)
+        for h in range(3):
             v = acc[rows, pl.ds(1152 + h * 128, 128)] * scale
             kvb[c, pl.ds(3 * CH, CH), pl.ds(384 + h * 128, 128)] = v.astype(BF16)
+        send_kv(c, 1)
 
     def finish_q(c):
         rows = pl.ds(c * CH, CH)
@@ -372,32 +341,36 @@
                 u = acc[rows, pl.ds((2 * h + g) * 128, 128)] * scale
                 qs[c, h, pl.ds(g * CH, CH), :] = head(u, gq[...].reshape(1, 128), c)
 
-    for c in range(NC):
-        @pl.loop(0, 2)
-        def _(h):
-            z_copy(c, h).wait_recv()
-            f_copy(c, h).start()
-            step(2, c, h)
-            f_copy(c, h).wait_recv()
-            step(3, c, h)
-
-        finish(c)
-        for ahead in (1, 3):
-            send_kv(ahead, c)
-            send_values(ahead, c)
-            if c != 1:
-                send_keys(ahead, c)
-        if c == 1:
-            relay_on(0, seq != 16)
-        if c == 2:
-            for ahead in (1, 3):
-                send_keys(ahead, 1)
-            for early in (0, 1):
-                for ahead in (1, 3):
-                    pass_values(ahead, early)
-            relay_on(0, seq == 16)
-            relay_back(0)
-        finish_q(c)
+    def z_step(c, h):
+        z_copy(c, h).wait_recv()
+        f_copy(c, h).start()
+        step(2, c, h)
+        f_copy(c, h).wait_recv()
+        step(3, c, h)
+
+    soon = (seq4 != 0) & jnp.logical_not(after_half)
+    z_step(0, 0)
+    z_step(0, 1)
+    finish(0)
+    finish_q(0)
+    z_step(1, 0)
+    relay_on(0, seq != 16)
+    relay_back(0, seq != 17)
+    z_step(1, 1)
+    finish(1)
+    finish_q(1)
+    z_step(2, 0)
+    relay_back(1, soon)
+    z_step(2, 1)
+    finish(2)
+    for ahead in (3, 1):
+        when(crosses(ahead, 1), kv_copy(0, ahead, 1, 0).start)
+    for c in (0, 1):
+        for ahead in (3, 1):
+            pass_values(ahead, c)
+    relay_on(0, seq == 16)
+    relay_back(0, seq == 17)
+    finish_q(2)
 
     def unit(c, cc):
         start = 0 if cc > c else CH
@@ -412,11 +385,11 @@
             o_acc[c, h] += jnp.dot(w.astype(BF16), vals, preferred_element_type=F32)
 
     relay_on(1)
-    relay_back(1)
+    relay_back(1, jnp.logical_not(soon))
     kv_arrived(0)
     for c in range(NC):
         unit(c, 0)
-    for ahead in (1, 3):
+    for ahead in (3, 1):
         pass_values(ahead, 2)
     relay_on(2)
     relay_back(2)
@@ -584,8 +557,8 @@
             dma, dma, dma,
             dma((NC, 2)), dma((NC, 2)), dma((NC, 2)), dma((NC, 2)),
             dma((3, 4)), dma((2,)), dma((2,)), dma((2,)),
-            dma((4, NC)), dma((3, NC)),
-            dma((2, NC)), dma((2, NC)), dma((2, NC)), dma((2, NC)),
+            dma((4, NC, 2)), dma((3, NC, 2)),
+            dma((2, NC)), dma((2, NC)), dma((2, NC)),
             dma((NC,)), dma((NC,)), dma((NC,)), dma((NC,)),
             dma((NC, 3)), dma((NC, 3)), dma((2, NC)),
         ],

time: 95.9 us -> 92 us (0.959)
  the two profiles are of different devices: /device:TPU:65 before, /device:TPU:99 now
where the time goes in v4:
time: 92 us; the launch traced here: 91.8 us
  Pallas kernels  91 us (99%)
    pallas_call x1, Pallas kernels, local(): pl.pallas_call(kernel, out_shape=(out, out), in_specs=[hbm, vmem, hbm, hb...  88.4 us
    pallas_call x1, Pallas kernels, local(): pl.pallas_call(copy_out, out_shape=(out, out), in_specs=[hbm, hbm], out_s...  2.51 us

profile of v4, /device:TPU:99, one launch (start us, length us, event | category | flops | bytes accessed | tf_op | source)
XLA Modules:
  0.0 91.8 jit_solution(17139476185045816957)
XLA Ops:
  0.6 88.4 %shard_map.122 = (bf16[1344,384]{1,0:T(8,128)(2,1)}, bf16[1344,384]{1,0:T(8,128)(2,1)}) custom-call(bf16[1344,384]{1,0:T(8,128)(2,1)} %bitcast.3, s32[384]{0:T(512)} %pos.1, bf16[5376,768]{1,0:T(8,128)(2,1)} %wq.1, bf16[5376,384]{1,0:T(8,128)(2,1)} %wk.1, bf16[5376,384]{1,0:T(8,128)(2,1)} %wv.1, bf16[768,5376]{1,0:T(8,128)(2,1)} %wo.1, f32[5376]{0:T(1024)} %gi.1, ...), custom_call_target="tpu_custom_call" | custom-call | flops 12000000000 | bytes 28000000 | tf_op jit(solution)/shard_map/pallas_call | solution.py:524
  89.1 2.5 %shard_map.123 = (bf16[1344,384]{1,0:T(8,128)(2,1)}, bf16[1344,384]{1,0:T(8,128)(2,1)}) custom-call(bf16[1344,384]{1,0:T(8,128)(2,1)} %get-tuple-element.6.hidden, bf16[1344,384]{1,0:T(8,128)(2,1)} %get-tuple-element.7.ffn_input), custom_call_target="tpu_custom_call" | custom-call | tf_op jit(solution)/shard_map/pallas_call | solution.py:582

commit v5 on v4

--- a/solution.py
+++ b/solution.py
@@ -120,7 +120,6 @@
         )
 
     seq4 = lax.rem(seq, 4)
-    seq16 = lax.rem(seq, 16)
     before_half = (seq >= 13) & (seq < 16)
     after_half = (seq >= 16) & (seq < 19)
 
@@ -154,12 +153,12 @@
     def crossed(ahead, c):
         return seq == 16 if ahead == 1 else after_half & gets(3, c)
 
-    def relays_on(c):
+    def relays_on(c, part):
         on = (seq >= 1) & (seq < N_SEQ - 1)
-        return on & (seq4 != 3) if c == 0 else on & (seq16 == 14)
-
-    def relays_back(c):
-        return (seq >= 3) & (seq4 == 1) if c == 0 else (seq >= 3) & (seq16 != 0)
+        return on & (seq4 != 3) if c == 0 or part == 0 else on & (seq4 == 2)
+
+    def relays_back(c, part):
+        return (seq >= 3) & (seq4 == 1) if c == 0 or part == 0 else (seq >= 3) & (seq4 != 0)
 
     def when(condition, action):
         @pl.when(condition)
@@ -169,13 +168,13 @@
     def send_kv(c, part):
         for ahead in (3, 1):
             across = crosses(ahead, c)
-            if part == 0 and c == 1:
-                when(sends(ahead, c) & jnp.logical_not(across), kv_copy(0, ahead, c, 0).start)
-            elif part == 0:
+            if part == 0:
                 when(sends(ahead, c), kv_copy(0, ahead, c, 0).start)
             else:
-                when(sends(ahead, c) & jnp.logical_not(across), kv_copy(0, ahead, c, 1).start)
-                when(across, value_copy(ahead, c).start)
+                straight = jnp.logical_not(across) if c < 2 else True
+                when(sends(ahead, c) & straight, kv_copy(0, ahead, c, 1).start)
+                if c < 2:
+                    when(across, value_copy(ahead, c).start)
 
     def pass_values(ahead, c):
         def act():
@@ -184,36 +183,36 @@
 
         when(crossed(ahead, c), act)
 
-    def relay(relays, back, ahead, c, some):
+    def relay(relays, back, ahead, c, part, some):
         def act():
-            for part in (0, 1):
-                kv_copy(0, back, c, part).wait_recv()
-                kv_copy(back, ahead, c, part).start()
-
-        when(relays(c) & some, act)
-
-    def relay_on(c, some=True):
-        relay(relays_on, 1, 1, c, some)
-
-    def relay_back(c, some=True):
-        relay(relays_back, 3, N_SEQ - 1, c, some)
+            kv_copy(0, back, c, part).wait_recv()
+            kv_copy(back, ahead, c, part).start()
+
+        when(relays(c, part) & some, act)
+
+    def relay_both(c, some_on=True, some_back=True):
+        for part in (0, 1):
+            relay(relays_on, 1, 1, c, part, some_on)
+            relay(relays_back, 3, N_SEQ - 1, c, part, some_back)
 
     def kv_arrived(c):
         for part in (0, 1):
-            when((seq >= 1) & jnp.logical_not(relays_on(c)), kv_copy(0, 1, c, part).wait_recv)
+            when((seq >= 1) & jnp.logical_not(relays_on(c, part)), kv_copy(0, 1, c, part).wait_recv)
             when(seq >= 2, kv_copy(1, 1, c, part).wait_recv)
-            when(gets(3, c) & jnp.logical_not(relays_back(c)), kv_copy(0, 3, c, part).wait_recv)
+            when(gets(3, c) & jnp.logical_not(relays_back(c, part)), kv_copy(0, 3, c, part).wait_recv)
 
     def kv_left(c):
         for ahead in (1, 3):
             across = crosses(ahead, c)
             when(sends(ahead, c), kv_copy(0, ahead, c, 0).wait_send)
-            when(sends(ahead, c) & jnp.logical_not(across), kv_copy(0, ahead, c, 1).wait_send)
-            when(across, value_copy(ahead, c).wait_send)
-            when(crossed(ahead, c), value_pass(ahead, c).wait_send)
+            straight = jnp.logical_not(across) if c < 2 else True
+            when(sends(ahead, c) & straight, kv_copy(0, ahead, c, 1).wait_send)
+            if c < 2:
+                when(across, value_copy(ahead, c).wait_send)
+                when(crossed(ahead, c), value_pass(ahead, c).wait_send)
         for part in (0, 1):
-            when(relays_on(c), kv_copy(1, 1, c, part).wait_send)
-            when(relays_back(c), kv_copy(3, N_SEQ - 1, c, part).wait_send)
+            when(relays_on(c, part), kv_copy(1, 1, c, part).wait_send)
+            when(relays_back(c, part), kv_copy(3, N_SEQ - 1, c, part).wait_send)
 
     def att_copy(c):
         return remote(
@@ -354,22 +353,18 @@
     finish(0)
     finish_q(0)
     z_step(1, 0)
-    relay_on(0, seq != 16)
-    relay_back(0, seq != 17)
+    relay_both(0, seq != 16, seq != 17)
     z_step(1, 1)
     finish(1)
     finish_q(1)
     z_step(2, 0)
-    relay_back(1, soon)
+    relay_both(1, soon, soon)
     z_step(2, 1)
     finish(2)
-    for ahead in (3, 1):
-        when(crosses(ahead, 1), kv_copy(0, ahead, 1, 0).start)
     for c in (0, 1):
         for ahead in (3, 1):
             pass_values(ahead, c)
-    relay_on(0, seq == 16)
-    relay_back(0, seq == 17)
+    relay_both(0, seq == 16, seq == 17)
     finish_q(2)
 
     def unit(c, cc):
@@ -384,15 +379,11 @@
             l_acc[c, h] += w[:, 0:128] + w[:, 128:256] + w[:, 256:384]
             o_acc[c, h] += jnp.dot(w.astype(BF16), vals, preferred_element_type=F32)
 
-    relay_on(1)
-    relay_back(1, jnp.logical_not(soon))
+    relay_both(1, jnp.logical_not(soon), jnp.logical_not(soon))
     kv_arrived(0)
     for c in range(NC):
         unit(c, 0)
-    for ahead in (3, 1):
-        pass_values(ahead, 2)
-    relay_on(2)
-    relay_back(2)
+    relay_both(2)
     kv_arrived(1)
     for c in range(NC):
         unit(c, 1)
@@ -441,7 +432,7 @@
                 for a, u, v in zip(sums, (s, t, t, sg), (s, t, sg, sg))
             )
 
-        sums = lax.fori_loop(0, OWN // BLOCK, one, (jnp.zeros((8, CH), F32),) * 4)
+        sums = lax.fori_loop(0, OWN // BLOCK, one, (jnp.zeros((8, CH), F32),) * 4, unroll=3)
         for i, v in enumerate(sums):
             st_send[c, pl.ds(i, 1), :] = jnp.sum(v, axis=0, keepdims=True)
         for i in range(4, 8):
@@ -458,7 +449,7 @@
         square = rows4[1:2] + 2.0 * post * rows4[2:3] + post * post * rows4[3:4]
         pre = lax.rsqrt(jnp.maximum(square, 0.0) / WIDTH + EPS)
 
-        @pl.loop(0, OWN // BLOCK)
+        @pl.loop(0, OWN // BLOCK, unroll=3)
         def _(i):
             rows = pl.ds(pl.multiple_of(i * BLOCK, BLOCK), BLOCK)
             t = xg[0, rows, cols].astype(F32)

time: 92 us -> 89.4 us (0.972)
  the two profiles are of different devices: /device:TPU:99 before, /device:TPU:65 now
where the time goes in v5:
time: 89.4 us; the launch traced here: 89.2 us
  Pallas kernels  88.4 us (99%)
    pallas_call x1, Pallas kernels, local(): pl.pallas_call(kernel, out_shape=(out, out), in_specs=[hbm, vmem, hbm, hb...  85.9 us
    pallas_call x1, Pallas kernels, local(): pl.pallas_call(copy_out, out_shape=(out, out), in_specs=[hbm, hbm], out_s...  2.51 us

profile of v5, /device:TPU:65, one launch (start us, length us, event | category | flops | bytes accessed | tf_op | source)
XLA Modules:
  0.0 89.2 jit_solution(11406891466481694702)
XLA Ops:
  0.6 85.9 %shard_map.122 = (bf16[1344,384]{1,0:T(8,128)(2,1)}, bf16[1344,384]{1,0:T(8,128)(2,1)}) custom-call(bf16[1344,384]{1,0:T(8,128)(2,1)} %bitcast.3, s32[384]{0:T(512)} %pos.1, bf16[5376,768]{1,0:T(8,128)(2,1)} %wq.1, bf16[5376,384]{1,0:T(8,128)(2,1)} %wk.1, bf16[5376,384]{1,0:T(8,128)(2,1)} %wv.1, bf16[768,5376]{1,0:T(8,128)(2,1)} %wo.1, f32[5376]{0:T(1024)} %gi.1, ...), custom_call_target="tpu_custom_call" | custom-call | flops 12000000000 | bytes 28000000 | tf_op jit(solution)/shard_map/pallas_call | solution.py:515
  86.5 2.5 %shard_map.123 = (bf16[1344,384]{1,0:T(8,128)(2,1)}, bf16[1344,384]{1,0:T(8,128)(2,1)}) custom-call(bf16[1344,384]{1,0:T(8,128)(2,1)} %get-tuple-element.6.hidden, bf16[1344,384]{1,0:T(8,128)(2,1)} %get-tuple-element.7.ffn_input), custom_call_target="tpu_custom_call" | custom-call | tf_op jit(solution)/shard_map/pallas_call | solution.py:573

commit v6 on v5

--- a/solution.py
+++ b/solution.py
@@ -155,9 +155,13 @@
 
     def relays_on(c, part):
         on = (seq >= 1) & (seq < N_SEQ - 1)
+        if c == 2 and part == 1:
+            return on & (seq4 >= 2)
         return on & (seq4 != 3) if c == 0 or part == 0 else on & (seq4 == 2)
 
     def relays_back(c, part):
+        if c == 2 and part == 1:
+            return (seq >= 3) & (seq4 >= 2)
         return (seq >= 3) & (seq4 == 1) if c == 0 or part == 0 else (seq >= 3) & (seq4 != 0)
 
     def when(condition, action):
@@ -396,6 +400,10 @@
     def project(c, i):
         return jnp.dot(att[pl.ds(c * CH, CH), :], wov[i], preferred_element_type=F32)
 
+    def project_half(c, i, part):
+        cols = pl.ds(part * KV, KV)
+        return jnp.dot(att[pl.ds(c * CH, CH), cols], wov[i, cols, :], preferred_element_type=F32)
+
     for c in range(NC):
         unit(c, 2)
         for h in range(3):
@@ -404,13 +412,10 @@
             att[pl.ds(c * CH, CH), pl.ds(2 * h * 128, 128)] = o[:CH]
             att[pl.ds(c * CH, CH), pl.ds((2 * h + 1) * 128, 128)] = o[CH:]
         att_copy(c).start()
-        if c > 0:
-            att_copy(c - 1).wait_recv()
-            rs_send[c - 1] = own_rows(project(c - 1, 0))[...].astype(BF16)
-            rs_copy(c - 1).start()
-    att_copy(2).wait_recv()
-    rs_send[2] = own_rows(project(2, 0))[...].astype(BF16)
-    rs_copy(2).start()
+        first = project_half(c, 0, 0)
+        att_copy(c).wait_recv()
+        rs_send[c] = own_rows(first + project_half(c, 0, 1))[...].astype(BF16)
+        rs_copy(c).start()
 
     for c in range(NC):
         own[c] = own_rows(project(c, 1))[...]

time: 89.4 us -> 87.1 us (0.974)
  Pallas kernels: 88.4 us -> 86.1 us
    pallas_call x1, Pallas kernels: 85.9 us -> 83.6 us  [local(): pl.pallas_call(kernel, out_shape=(out, out), in_specs=[hbm, vmem, hbm, hb...]
where the time goes in v6:
time: 87.1 us; the launch traced here: 86.9 us
  Pallas kernels  86.1 us (99%)
    pallas_call x1, Pallas kernels, local(): pl.pallas_call(kernel, out_shape=(out, out), in_specs=[hbm, vmem, hbm, hb...  83.6 us
    pallas_call x1, Pallas kernels, local(): pl.pallas_call(copy_out, out_shape=(out, out), in_specs=[hbm, hbm], out_s...  2.51 us

profile of v6, /device:TPU:65, one launch (start us, length us, event | category | flops | bytes accessed | tf_op | source)
XLA Modules:
  0.0 86.9 jit_solution(11483124138873958665)
XLA Ops:
  0.6 83.6 %shard_map.122 = (bf16[1344,384]{1,0:T(8,128)(2,1)}, bf16[1344,384]{1,0:T(8,128)(2,1)}) custom-call(bf16[1344,384]{1,0:T(8,128)(2,1)} %bitcast.3, s32[384]{0:T(512)} %pos.1, bf16[5376,768]{1,0:T(8,128)(2,1)} %wq.1, bf16[5376,384]{1,0:T(8,128)(2,1)} %wk.1, bf16[5376,384]{1,0:T(8,128)(2,1)} %wv.1, bf16[768,5376]{1,0:T(8,128)(2,1)} %wo.1, f32[5376]{0:T(1024)} %gi.1, ...), custom_call_target="tpu_custom_call" | custom-call | flops 12000000000 | bytes 28000000 | tf_op jit(solution)/shard_map/pallas_call | solution.py:520
  84.2 2.5 %shard_map.123 = (bf16[1344,384]{1,0:T(8,128)(2,1)}, bf16[1344,384]{1,0:T(8,128)(2,1)}) custom-call(bf16[1344,384]{1,0:T(8,128)(2,1)} %get-tuple-element.6.hidden, bf16[1344,384]{1,0:T(8,128)(2,1)} %get-tuple-element.7.ffn_input), custom_call_target="tpu_custom_call" | custom-call | tf_op jit(solution)/shard_map/pallas_call | solution.py:578

commit v7 on v6

--- a/solution.py
+++ b/solution.py
@@ -24,6 +24,7 @@
 NC = 3
 KV = 768
 N_SEQ = 32
+PIECES = (((0, 672), (672, 672)), ((0, 672), (672, 672)), ((0, 672), (672, 336), (1008, 336)))
 SCORE = 168.0**-0.5 * math.log2(math.e)
 
 
@@ -81,7 +82,7 @@
         )
 
     def piece(ref, c, h):
-        return ref.at[pl.ds(h * HALF, HALF), pl.ds(c * CH, CH)]
+        return ref.at[pl.ds(*PIECES[c][h]), pl.ds(c * CH, CH)]
 
     def z_copy(c, h):
         return remote(piece(xt, c, h), piece(xg.at[2], c, h), s_z.at[c, h], r_z.at[c, h], peer(2))
@@ -239,7 +240,7 @@
             cp.start()
     pl.semaphore_wait(barrier, partners)
     for c in range(NC):
-        for h in range(2):
+        for h in range(len(PIECES[c])):
             z_copy(c, h).start()
     sib_copy.start()
     for k in (2, 3):
@@ -291,12 +292,12 @@
 
     own_copy.wait()
 
-    def step(k, c, h):
+    def step(k, c, h, part=(0, HALF)):
         cols = pl.ds(pl.multiple_of(c * CH, CH), CH)
-        feats = pl.ds(pl.multiple_of(h * HALF, 16), HALF)
+        feats = pl.ds(pl.multiple_of(h * HALF + part[0], 16), part[1])
         x = xg[k, feats, cols].astype(F32)
         ss[c] += jnp.broadcast_to(jnp.sum(x * x, axis=0, keepdims=True), (8, CH))
-        gain = gtab[tp_of(k) * 2 + h, pl.ds(0, 1), :]
+        gain = gtab[tp_of(k) * 2 + h, pl.ds(0, 1), :][:, part[0] : part[0] + part[1]]
         x = (x.T * gain).astype(BF16)
         acc[cols, pl.ds(0, 768)] += jnp.dot(x, wqv[k, feats, :], preferred_element_type=F32)
         acc[cols, pl.ds(768, 384)] += jnp.dot(x, wkv[k, feats, :], preferred_element_type=F32)
@@ -347,9 +348,11 @@
     def z_step(c, h):
         z_copy(c, h).wait_recv()
         f_copy(c, h).start()
-        step(2, c, h)
+        first, size = PIECES[c][h]
+        place = (c, first // HALF, (first % HALF, size))
+        step(2, *place)
         f_copy(c, h).wait_recv()
-        step(3, c, h)
+        step(3, *place)
 
     soon = (seq4 != 0) & jnp.logical_not(after_half)
     z_step(0, 0)
@@ -364,6 +367,7 @@
     z_step(2, 0)
     relay_both(1, soon, soon)
     z_step(2, 1)
+    z_step(2, 2)
     finish(2)
     for c in (0, 1):
         for ahead in (3, 1):
@@ -480,7 +484,7 @@
 
     sib_copy.wait_send()
     for c in range(NC):
-        for h in range(2):
+        for h in range(len(PIECES[c])):
             z_copy(c, h).wait_send()
             f_copy(c, h).wait_send()
         for k in (1, 2, 3):
@@ -551,7 +555,7 @@
             pltpu.VMEM((NC, 3, 8, CH), F32),
             pltpu.VMEM((2, NC, CH, 384), BF16),
             dma, dma, dma,
-            dma((NC, 2)), dma((NC, 2)), dma((NC, 2)), dma((NC, 2)),
+            dma((NC, 3)), dma((NC, 3)), dma((NC, 3)), dma((NC, 3)),
             dma((3, 4)), dma((2,)), dma((2,)), dma((2,)),
             dma((4, NC, 2)), dma((3, NC, 2)),
             dma((2, NC)), dma((2, NC)), dma((2, NC)),

time: 87.1 us -> 87.7 us (level)
  no operation moved by 1% of the time
where the time goes in v7:
time: 87.7 us; the launch traced here: 87.1 us
  Pallas kernels  86.3 us (98%)
    pallas_call x1, Pallas kernels, local(): pl.pallas_call(kernel, out_shape=(out, out), in_specs=[hbm, vmem, hbm, hb...  83.8 us
    pallas_call x1, Pallas kernels, local(): pl.pallas_call(copy_out, out_shape=(out, out), in_specs=[hbm, hbm], out_s...  2.51 us

profile of v7, /device:TPU:65, one launch (start us, length us, event | category | flops | bytes accessed | tf_op | source)
XLA Modules:
  0.0 87.1 jit_solution(5115614430250770634)
XLA Ops:
  0.6 83.8 %shard_map.122 = (bf16[1344,384]{1,0:T(8,128)(2,1)}, bf16[1344,384]{1,0:T(8,128)(2,1)}) custom-call(bf16[1344,384]{1,0:T(8,128)(2,1)} %bitcast.3, s32[384]{0:T(512)} %pos.1, bf16[5376,768]{1,0:T(8,128)(2,1)} %wq.1, bf16[5376,384]{1,0:T(8,128)(2,1)} %wk.1, bf16[5376,384]{1,0:T(8,128)(2,1)} %wv.1, bf16[768,5376]{1,0:T(8,128)(2,1)} %wo.1, f32[5376]{0:T(1024)} %gi.1, ...), custom_call_target="tpu_custom_call" | custom-call | flops 12000000000 | bytes 28000000 | tf_op jit(solution)/shard_map/pallas_call | solution.py:524
  84.4 2.5 %shard_map.123 = (bf16[1344,384]{1,0:T(8,128)(2,1)}, bf16[1344,384]{1,0:T(8,128)(2,1)}) custom-call(bf16[1344,384]{1,0:T(8,128)(2,1)} %get-tuple-element.6.hidden, bf16[1344,384]{1,0:T(8,128)(2,1)} %get-tuple-element.7.ffn_input), custom_call_target="tpu_custom_call" | custom-call | tf_op jit(solution)/shard_map/pallas_call | solution.py:582
